TPU v7x, 32 devices: a whole 2x2x4 slice. The times are simulated.
32 devices in a mesh: groups: 2 (over y), tensor: 4 (over z), section: 4 (over x, core).
Axes of the slice: x: 2, y: 2, z: 4, core: 2. Of those that a mesh axis runs over, the one named last changes fastest.
Arguments:
- prefill_x: bfloat16 [4096, 8192], P(('groups', 'section'), 'tensor'), parts along dimension 0, may hold values from -6 to 6
- norm_gain: float32 [8192], replicated, may hold values from 0.5 to 2
- w_q: bfloat16 [8192, 8192], P(None, 'tensor'), may hold values from -127 to 127, as said below
- q_scale: float32 [8192], P('tensor'), may hold values from 7.7339806e-05 to 0.00030935922
- key_value_weight: bfloat16 [8192, 2048], P(None, 'tensor'), may hold values from -127 to 127, as said below
- key_value_scale: float32 [2048], P('tensor'), may hold values from 7.7339806e-05 to 0.00030935922
- w_o: bfloat16 [8192, 8192], P('tensor'), may hold values from -127 to 127, as said below
- o_scale: float32 [8192], P('tensor'), may hold values from 0.0022097088 to 0.008838835
- prefix_cache: bfloat16 [4, 32, 2048, 512], P('tensor', ('groups', 'section')), parts along dimension 1, may hold values from -2048 to 2048, as said below
- prefix_len: int32 [32], P(('groups', 'section')), parts along dimension 0, may hold values from 512 to 2048, as said below
- dec_x: bfloat16 [2, 256, 8192], P(None, ('groups', 'section'), 'tensor'), parts along dimension 1, may hold values from -6 to 6
- dec_cache: bfloat16 [4, 256, 64, 512], P('tensor', ('groups', 'section')), parts along dimension 1, may hold values from -2048 to 2048, as said below
- dec_len: int32 [256], P(('groups', 'section')), parts along dimension 0, may hold values from 16 to 64, as said below
- place: int32 [32], P('groups'), parts along dimension 0, may hold values from 0 to 127, as said below
Outputs:
- prefill_out: bfloat16 [4096, 8192], P(('groups', 'section'), 'tensor'), parts along dimension 0
- decode_out: bfloat16 [2, 256, 8192], P(None, ('groups', 'section'), 'tensor'), parts along dimension 1
There are 2 independent parts, one for each index of `groups`. A program takes and returns all parts, laid end to end along the dimension named above; an argument that names none is the same for every part. Nothing has to cross between parts.
Inputs may be any that keep to these rules, and one draw needn't show every extreme that they name: `w_q`: integers, int8 weight values. `key_value_weight`: integers, int8 weight values. `w_o`: integers, int8 weight values. `prefix_cache`: copies of one kv head on different tensor indices are equal. `dec_cache`: copies of one kv head on different tensor indices are equal. `prefix_len`: some prompt has exactly 2048 live positions. `dec_len`: some decode row has exactly 64 live positions. place[s * 4 + p] = o * 32 + r sends prompt p of section index s to decode row r of owner section index o; no two prompts share a decode row; one section index sends at most 2 prompts to one owner, and in every draw some owner receives 2 prompts from every section index.
All inputs are finite; a program needn't handle non-finite values.
Results may differ from a plain program's by a relative error of at most 0.024.
Values may be sent and summed in bfloat16 or wider, within the bound.
No kernel may reach another device: no remote copies, remote signals or barrier semaphores. Data moves between devices by JAX's collectives and lax.ppermute only.
A program may use at most 192 MiB of HBM per device.

v0:
```python
import functools
import math

import jax
import jax.numpy as jnp
from jax import lax
from jax.experimental import pallas as pl
from jax.experimental.pallas import tpu as pltpu
from jax.sharding import PartitionSpec as P

HEAD_SIZE = 128
PROMPT_TOKENS = 128
KERNEL_VMEM = 46 << 20
WEIGHT_BUFFERS = 8
EXP2_FACTOR = math.log2(math.e) / math.sqrt(HEAD_SIZE)
MASKED = -1e30


def partner_2(block, axis, distance):
    count = lax.axis_size(axis)
    route = []
    for low in range(count):
        high = low | 1 << distance
        if high != low and high < count:
            route += [(low, high), (high, low)]
    return lax.ppermute(block, axis, route)


def joined(portion, partner, bit_number, concat_dim, tensor_index):
    upper_half = tensor_index // 2**bit_number % 2 == 1
    lower_first = jnp.concatenate([portion, partner], axis=concat_dim)
    upper_first = jnp.concatenate([partner, portion], axis=concat_dim)
    return jnp.where(upper_half, upper_first, lower_first)


def tile_of(extent, most):
    tile = extent
    while tile > most and tile % 2 == 0:
        tile //= 2
    return tile


def after(value, *others):
    return lax.optimization_barrier((value,) + others)[0]


def after_all(values, *others):
    return lax.optimization_barrier(tuple(values) + others)[: len(values)]


def line_order(index):
    low = index < 2
    return [index, index ^ 1, jnp.where(low, 2, 1), jnp.where(low, 3, 0)]


OUTER = [(0, 1), (1, 0), (2, 3), (3, 2)]
MIDDLE = [(1, 2), (2, 1)]
INWARD = [(0, 1), (3, 2)]
OUTWARD = [(1, 0), (2, 3)]


class LineGather:
    def __init__(self, block, axis, outer_held=(), middle_held=()):
        self.block, self.axis = block, axis
        self.partner = lax.ppermute(after(block, *outer_held), axis, OUTER)
        self.middle = lax.ppermute(after(block, *middle_held), axis, MIDDLE)

    def second(self, *held):
        partner, middle = after_all((self.partner, self.middle), *held)
        self.outer = lax.ppermute(middle, self.axis, OUTWARD)
        self.middle_far = lax.ppermute(partner, self.axis, MIDDLE)

    def third(self, *held):
        self.outer_far = lax.ppermute(after(self.middle_far, *held), self.axis, OUTWARD)

    def slots(self):
        return [
            [self.block],
            [self.partner],
            [self.middle, self.outer],
            [self.middle_far, self.outer_far],
        ]


def added(*terms):
    total = sum(term.astype(jnp.float32) for term in terms)
    return total.astype(terms[0].dtype)


class LineScatter:
    def __init__(self, own, partner, near, far, axis):
        self.own, self.partner, self.near, self.far = own, partner, near, far
        self.axis = axis
        self.far_in = lax.ppermute(far, axis, INWARD)

    def second(self, *held):
        far, near = after_all((added(self.far, self.far_in), self.near), *held)
        self.first_hop = (far,)
        self.near_in = lax.ppermute(near, self.axis, INWARD)
        self.far_out = lax.ppermute(far, self.axis, MIDDLE)

    def third(self, *held):
        near, partner = after_all(
            (added(self.near, self.near_in), added(self.partner, self.far_out)), *held
        )
        self.second_hop = (near, partner)
        near = lax.ppermute(near, self.axis, MIDDLE)
        partner = lax.ppermute(partner, self.axis, OUTER)
        self.terms = [self.own, near, partner]


def qkv_kernel(counts, begun, ended, tile, order, *refs):
    refs = list(refs)
    arrays = sum(counts)
    xs = [refs.pop(0) for _ in range(arrays)]
    gain_ref, wq_ref, wkv_ref = (refs.pop(0) for _ in range(3))
    sums_in = [refs.pop(0) for _ in range(3)] if begun else []
    if ended:
        qs_ref, kvs_ref, q_ref, kv_ref, accq, acckv, squares = (refs.pop(0) for _ in range(7))
    else:
        accq, acckv, squares = (refs.pop(0) for _ in range(3))
    x_bufs = [refs.pop(0) for _ in range(arrays)]
    wq_buf, wkv_buf, x_sem, w_sem, sum_sem = refs
    per = x_bufs[0].shape[1] // tile
    steps = len(counts) * per
    ahead = min(steps, wq_buf.shape[0])

    def weight_copies(step):
        buffer = lax.rem(step, ahead)
        at = pl.multiple_of((order[step // per] * per + lax.rem(step, per)) * tile, tile)
        return [
            pltpu.make_async_copy(ref.at[pl.ds(at, tile)], buf.at[buffer], w_sem.at[w, buffer])
            for w, (ref, buf) in enumerate([(wq_ref, wq_buf), (wkv_ref, wkv_buf)])
        ]

    x_copies = [
        pltpu.make_async_copy(ref, buf, x_sem.at[a]) for a, (ref, buf) in enumerate(zip(xs, x_bufs))
    ]
    sum_copies = [
        pltpu.make_async_copy(ref, acc, sum_sem.at[a])
        for a, (ref, acc) in enumerate(zip(sums_in, (accq, acckv, squares)))
    ]
    for copy in x_copies[: counts[0]] + sum_copies:
        copy.start()
    for step in range(ahead):
        for copy in weight_copies(step):
            copy.start()
    for copy in x_copies[counts[0] :]:
        copy.start()
    for copy in sum_copies:
        copy.wait()
    if not begun:
        accq[...] = jnp.zeros_like(accq)
        acckv[...] = jnp.zeros_like(acckv)
        squares[...] = jnp.zeros_like(squares)

    taken = 0
    for s, count in enumerate(counts):
        for copy in x_copies[taken : taken + count]:
            copy.wait()
        bufs = x_bufs[taken : taken + count]
        taken += count

        def body(j, carry, s=s, bufs=bufs):
            step = s * per + j
            for copy in weight_copies(step):
                copy.wait()
            at = pl.multiple_of(j * tile, tile)
            values = sum(buf[:, pl.ds(at, tile)].astype(jnp.float32) for buf in bufs)
            gain = gain_ref[:, pl.ds(pl.multiple_of((order[s] * per + j) * tile, tile), tile)]
            squares[...] += jnp.broadcast_to(
                jnp.sum(values * values, axis=-1, keepdims=True), squares.shape
            )
            scaled = (values * gain).astype(jnp.bfloat16)
            buffer = lax.rem(step, ahead)
            accq[...] += jnp.dot(scaled, wq_buf[buffer], preferred_element_type=jnp.float32)
            acckv[...] += jnp.dot(scaled, wkv_buf[buffer], preferred_element_type=jnp.float32)

            @pl.when(step + ahead < steps)
            def _():
                for copy in weight_copies(step + ahead):
                    copy.start()

            return carry

        lax.fori_loop(0, per, body, 0)
    if ended:
        root = lax.rsqrt(squares[:, :1] / ended + 1e-05)
        q_ref[...] = (accq[...] * root * qs_ref[...]).astype(q_ref.dtype)
        kv_ref[...] = (acckv[...] * root * kvs_ref[...]).astype(kv_ref.dtype)


def project_part(slots, order, norm_gain, w_q, kv_weight, begun, scales):
    rows, depth = slots[0][0].shape
    tile = tile_of(depth, 512)
    q_cols, kv_cols = w_q.shape[1], kv_weight.shape[1]
    arrays = [array for slot in slots for array in slot]

    def whole(shape):
        return pl.BlockSpec(shape, lambda g, order: (0,) * len(shape))

    anywhere = pl.BlockSpec(memory_space=pl.ANY)
    operands = arrays + [norm_gain.reshape(1, -1), w_q, kv_weight]
    in_specs = [anywhere] * len(arrays) + [whole((1, norm_gain.shape[0])), anywhere, anywhere]
    sums = [(rows, q_cols), (rows, kv_cols), (rows, HEAD_SIZE)]
    if begun is not None:
        operands += list(begun)
        in_specs += [anywhere] * 3
    if scales is not None:
        operands += [scale.reshape(1, -1) for scale in scales]
        in_specs += [whole((1, q_cols)), whole((1, kv_cols))]
        out_shapes = [jax.ShapeDtypeStruct(shape, jnp.bfloat16) for shape in sums[:2]]
        scratch = [pltpu.VMEM(shape, jnp.float32) for shape in sums]
    else:
        out_shapes = [jax.ShapeDtypeStruct(shape, jnp.float32) for shape in sums]
        scratch = []
    return pl.pallas_call(
        functools.partial(
            qkv_kernel,
            [len(slot) for slot in slots],
            begun is not None,
            0 if scales is None else w_q.shape[0],
            tile,
        ),
        grid_spec=pltpu.PrefetchScalarGridSpec(
            num_scalar_prefetch=1,
            grid=(1,),
            in_specs=in_specs,
            out_specs=[whole(out.shape) for out in out_shapes],
            scratch_shapes=scratch
            + [pltpu.VMEM((rows, depth), jnp.bfloat16) for _ in arrays]
            + [
                pltpu.VMEM((WEIGHT_BUFFERS, tile, q_cols), jnp.bfloat16),
                pltpu.VMEM((WEIGHT_BUFFERS, tile, kv_cols), jnp.bfloat16),
                pltpu.SemaphoreType.DMA((len(arrays),)),
                pltpu.SemaphoreType.DMA((2, WEIGHT_BUFFERS)),
                pltpu.SemaphoreType.DMA((3,)),
            ],
        ),
        out_shape=out_shapes,
        compiler_params=pltpu.CompilerParams(vmem_limit_bytes=KERNEL_VMEM),
        cost_estimate=pl.CostEstimate(
            flops=2 * rows * depth * len(slots) * (q_cols + kv_cols),
            bytes_accessed=2 * depth * len(slots) * (q_cols + kv_cols),
            transcendentals=0,
        ),
        name="norm_qkv",
    )(order, *operands)


def out_kernel(count, stacked, tile, order, x_ref, w_ref, *refs):
    if stacked:
        outs, refs = [refs[0].at[s] for s in range(count)], refs[1:]
    else:
        outs, refs = refs[:count], refs[count:]
    x_buf, w_buf, x_sem, w_sem, o_sem = refs[:5]
    o_bufs = refs[5:]
    per = o_bufs[0].shape[1] // tile
    steps = count * per
    ahead = min(steps, w_buf.shape[0])

    def weight_copy(step):
        at = pl.multiple_of((order[step // per] * per + lax.rem(step, per)) * tile, tile)
        buffer = lax.rem(step, ahead)
        return pltpu.make_async_copy(
            w_ref.at[:, pl.ds(at, tile)], w_buf.at[buffer], w_sem.at[buffer]
        )

    x_copy = pltpu.make_async_copy(x_ref, x_buf, x_sem)
    x_copy.start()
    for step in range(ahead):
        weight_copy(step).start()
    x_copy.wait()
    o_copies = []
    for s, (out, o_buf) in enumerate(zip(outs, o_bufs)):

        def body(j, carry, s=s, o_buf=o_buf):
            step = s * per + j
            weight_copy(step).wait()
            o_buf[:, pl.ds(pl.multiple_of(j * tile, tile), tile)] = jnp.dot(
                x_buf[...], w_buf[lax.rem(step, ahead)], preferred_element_type=jnp.float32
            ).astype(o_buf.dtype)

            @pl.when(step + ahead < steps)
            def _():
                weight_copy(step + ahead).start()

            return carry

        lax.fori_loop(0, per, body, 0)
        o_copies.append(pltpu.make_async_copy(o_buf, out, o_sem.at[s]))
        o_copies[-1].start()
    for copy in o_copies:
        copy.wait()


def without(kernel, first, count):
    return lambda *refs: kernel(*refs[:first], *refs[first + count :])


def project_out(attended, w_o, order, block, stacked=False, held=()):
    rows, depth = attended.shape
    tile = tile_of(block, 512)
    count = order.shape[0]
    anywhere = pl.BlockSpec(memory_space=pl.ANY)
    return pl.pallas_call(
        without(functools.partial(out_kernel, count, stacked, tile), 3, len(held)),
        grid_spec=pltpu.PrefetchScalarGridSpec(
            num_scalar_prefetch=1,
            grid=(1,),
            in_specs=[anywhere] * (2 + len(held)),
            out_specs=anywhere if stacked else [anywhere] * count,
            scratch_shapes=[
                pltpu.VMEM((rows, depth), jnp.bfloat16),
                pltpu.VMEM((WEIGHT_BUFFERS, depth, tile), jnp.bfloat16),
                pltpu.SemaphoreType.DMA,
                pltpu.SemaphoreType.DMA((WEIGHT_BUFFERS,)),
                pltpu.SemaphoreType.DMA((count,)),
            ]
            + [pltpu.VMEM((rows, block), jnp.bfloat16)] * count,
        ),
        out_shape=jax.ShapeDtypeStruct((count, rows, block), jnp.bfloat16)
        if stacked
        else [jax.ShapeDtypeStruct((rows, block), jnp.bfloat16)] * count,
        compiler_params=pltpu.CompilerParams(vmem_limit_bytes=KERNEL_VMEM),
        cost_estimate=pl.CostEstimate(
            flops=2 * rows * depth * count * block,
            bytes_accessed=2 * depth * count * block,
            transcendentals=0,
        ),
        name="project_out",
    )(order, attended, w_o, *held)


def with_ones(values):
    return jnp.concatenate([values, jnp.ones_like(values)], axis=1)


def scores_of(queries, keys):
    return lax.dot_general(
        queries, keys, (((1,), (1,)), ((), ())), preferred_element_type=jnp.float32
    )


def prefill_kernel(kv_heads, group, span, first, len_ref, q_ref, cache_ref, new_ref, o_ref, *scratch):
    accs, peaks = scratch[:kv_heads], scratch[kv_heads:]
    tokens = q_ref.shape[0]
    rows = group * tokens
    live = len_ref[first + pl.program_id(0)]
    full = live // span
    query_token = lax.rem(lax.broadcasted_iota(jnp.int32, (rows, tokens), 0), tokens)
    key_token = lax.broadcasted_iota(jnp.int32, (rows, tokens), 1)
    causal = key_token <= query_token
    lane = lax.broadcasted_iota(jnp.int32, (1, span), 1)

    def queries_of(a):
        return jnp.concatenate(
            [
                q_ref[:, (a * group + h) * HEAD_SIZE : (a * group + h + 1) * HEAD_SIZE]
                for h in range(group)
            ],
            axis=0,
        )

    def columns(a, part):
        return pl.ds((2 * a + part) * HEAD_SIZE, HEAD_SIZE)

    for a in range(kv_heads):
        scores = jnp.where(causal, scores_of(queries_of(a), new_ref[:, columns(a, 0)]), MASKED)
        top = jnp.broadcast_to(jnp.max(scores, axis=-1, keepdims=True), (rows, HEAD_SIZE))
        weights = jnp.exp2(scores - top[:, :tokens]).astype(jnp.bfloat16)
        accs[a][...] = jnp.dot(
            weights, with_ones(new_ref[:, columns(a, 1)]), preferred_element_type=jnp.float32
        )
        peaks[a][...] = top

    def block(s, bias):
        at = pl.multiple_of(s * span, span)
        scores = [
            scores_of(queries_of(a), cache_ref[0, 0, pl.ds(at, span), columns(a, 0)])
            for a in range(kv_heads)
        ]
        for a in range(kv_heads):
            here = scores[a] if bias is None else scores[a] + bias
            before = peaks[a][...]
            top = jnp.maximum(before, jnp.max(here, axis=-1, keepdims=True))
            weights = jnp.exp2(
                here - jnp.concatenate([top] * (span // HEAD_SIZE), axis=1)
            ).astype(jnp.bfloat16)
            fade = jnp.exp2(before - top)
            values = cache_ref[0, 0, pl.ds(at, span), columns(a, 1)]
            accs[a][...] = accs[a][...] * jnp.concatenate([fade, fade], axis=1) + jnp.dot(
                weights, with_ones(values), preferred_element_type=jnp.float32
            )
            peaks[a][...] = top

    def step(s, carry):
        block(s, None)
        return carry

    lax.fori_loop(0, full, step, 0)

    @pl.when(full * span < live)
    def _():
        block(full, jnp.where(lane + full * span < live, 0.0, MASKED))

    for a in range(kv_heads):
        result = accs[a][:, :HEAD_SIZE] / accs[a][:, HEAD_SIZE:]
        for h in range(group):
            o_ref[:, (a * group + h) * HEAD_SIZE : (a * group + h + 1) * HEAD_SIZE] = result[
                h * tokens : (h + 1) * tokens
            ].astype(o_ref.dtype)


def prefill_attention(queries, prefix_cache, first, count, new_kv, prefix_len):
    width = queries.shape[1]
    positions, page = prefix_cache.shape[2:]
    kv_heads = page // (2 * HEAD_SIZE)
    group = width // HEAD_SIZE // kv_heads
    span = tile_of(positions, 512)
    rows = group * PROMPT_TOKENS
    return pl.pallas_call(
        functools.partial(prefill_kernel, kv_heads, group, span, first),
        grid_spec=pltpu.PrefetchScalarGridSpec(
            num_scalar_prefetch=1,
            grid=(count,),
            in_specs=[
                pl.BlockSpec((PROMPT_TOKENS, width), lambda g, n: (g, 0)),
                pl.BlockSpec((1, 1, positions, page), lambda g, n: (0, first + g, 0, 0)),
                pl.BlockSpec((PROMPT_TOKENS, page), lambda g, n: (g, 0)),
            ],
            out_specs=pl.BlockSpec((PROMPT_TOKENS, width), lambda g, n: (g, 0)),
            scratch_shapes=[pltpu.VMEM((rows, 2 * HEAD_SIZE), jnp.float32)] * kv_heads
            + [pltpu.VMEM((rows, HEAD_SIZE), jnp.float32)] * kv_heads,
        ),
        out_shape=jax.ShapeDtypeStruct((count * PROMPT_TOKENS, width), jnp.bfloat16),
        compiler_params=pltpu.CompilerParams(vmem_limit_bytes=KERNEL_VMEM),
        cost_estimate=pl.CostEstimate(
            flops=8 * count * rows * kv_heads * (positions + PROMPT_TOKENS) * HEAD_SIZE,
            bytes_accessed=2 * count * positions * page,
            transcendentals=count * rows * kv_heads * (positions + PROMPT_TOKENS),
        ),
        name="prefill_attention",
    )(prefix_len, queries, prefix_cache, new_kv)


def decode_kernel(
    kv_heads, batch, len_ref, row_ref, q_ref, cache_ref, landed_ref, fresh_ref, o_ref, acc, peak
):
    row_count, context = cache_ref.shape[1], cache_ref.shape[2]
    per_row = q_ref.shape[2]
    steps = fresh_ref.shape[1]
    rows = batch * per_row
    row_of = lax.broadcasted_iota(jnp.int32, (rows, batch * context), 0) // per_row
    key_row = lax.broadcasted_iota(jnp.int32, (rows, batch * context), 1) // context
    key_at = lax.rem(lax.broadcasted_iota(jnp.int32, (rows, batch * context), 1), context)
    fresh_query = lax.broadcasted_iota(jnp.int32, (rows, batch * steps), 0)
    fresh_key = lax.broadcasted_iota(jnp.int32, (rows, batch * steps), 1)
    fresh_live = (fresh_key // steps == fresh_query // per_row) & (
        lax.rem(fresh_key, steps) <= lax.rem(fresh_query, per_row) // (per_row // steps)
    )

    def cached(b, carry):
        first = b * batch
        live = jnp.zeros_like(key_row)
        for r in range(batch):
            live = jnp.where(key_row == r, len_ref[first + r], live)
        cache_live = (row_of == key_row) & (key_at < live)
        pages = cache_ref[0, pl.ds(first, batch)].reshape(batch * context, cache_ref.shape[3])
        fresh = fresh_ref[pl.ds(first, batch)].reshape(batch * steps, fresh_ref.shape[2])
        for a in range(kv_heads):
            queries = q_ref[pl.ds(first, batch), a].reshape(rows, HEAD_SIZE).astype(jnp.bfloat16)
            k_at, v_at = 2 * a * HEAD_SIZE, (2 * a + 1) * HEAD_SIZE
            scores = scores_of(queries, pages[:, k_at : k_at + HEAD_SIZE])
            scores = jnp.where(cache_live, scores, MASKED)
            recent = scores_of(queries, fresh[:, k_at : k_at + HEAD_SIZE].astype(jnp.bfloat16))
            recent = jnp.where(fresh_live, recent, MASKED)
            top = jnp.maximum(
                jnp.max(scores, axis=-1, keepdims=True), jnp.max(recent, axis=-1, keepdims=True)
            )
            weights = jnp.exp2(scores - top).astype(jnp.bfloat16)
            recent = jnp.exp2(recent - top).astype(jnp.bfloat16)
            total = jnp.dot(
                weights,
                with_ones(pages[:, v_at : v_at + HEAD_SIZE]),
                preferred_element_type=jnp.float32,
            ) + jnp.dot(
                recent,
                with_ones(fresh[:, v_at : v_at + HEAD_SIZE].astype(jnp.bfloat16)),
                preferred_element_type=jnp.float32,
            )
            acc[pl.ds(first, batch), a] = total.reshape(batch, per_row, 2 * HEAD_SIZE)
            peak[pl.ds(first, batch), a] = jnp.broadcast_to(top, (rows, HEAD_SIZE)).reshape(
                batch, per_row, HEAD_SIZE
            )
        return carry

    lax.fori_loop(0, row_count // batch, cached, 0)

    def arrival(slot, carry):
        row = row_ref[slot]

        @pl.when(row >= 0)
        def _():
            for a in range(kv_heads):
                queries = q_ref[row, a].astype(jnp.bfloat16)
                k_at, v_at = 2 * a * HEAD_SIZE, (2 * a + 1) * HEAD_SIZE
                scores = scores_of(queries, landed_ref[slot, :, k_at : k_at + HEAD_SIZE])
                before = peak[row, a]
                top = jnp.maximum(before, jnp.max(scores, axis=-1, keepdims=True))
                weights = jnp.exp2(scores - top[:, :1]).astype(jnp.bfloat16)
                fade = jnp.exp2(before - top)
                acc[row, a] = acc[row, a] * jnp.concatenate([fade, fade], axis=1) + jnp.dot(
                    weights,
                    with_ones(landed_ref[slot, :, v_at : v_at + HEAD_SIZE]),
                    preferred_element_type=jnp.float32,
                )

        return carry

    lax.fori_loop(0, row_ref.shape[0], arrival, 0)
    o_ref[...] = (acc[:, :, :, :HEAD_SIZE] / acc[:, :, :, HEAD_SIZE:]).astype(o_ref.dtype)


def decode_attention(queries, dec_cache, dec_len, landed, slot_rows, fresh):
    row_count, kv_heads, per_row = queries.shape[:3]
    context = dec_cache.shape[2]
    batch = max(1, min(row_count, 2 * HEAD_SIZE // context))
    whole = lambda array: pl.BlockSpec(array.shape, lambda g, *_: (0,) * array.ndim)
    return pl.pallas_call(
        functools.partial(decode_kernel, kv_heads, batch),
        grid_spec=pltpu.PrefetchScalarGridSpec(
            num_scalar_prefetch=2,
            grid=(1,),
            in_specs=[whole(queries), whole(dec_cache), whole(landed), whole(fresh)],
            out_specs=whole(queries),
            scratch_shapes=[
                pltpu.VMEM((row_count, kv_heads, per_row, 2 * HEAD_SIZE), jnp.float32),
                pltpu.VMEM((row_count, kv_heads, per_row, HEAD_SIZE), jnp.float32),
            ],
        ),
        out_shape=jax.ShapeDtypeStruct(queries.shape, jnp.float32),
        compiler_params=pltpu.CompilerParams(vmem_limit_bytes=KERNEL_VMEM),
        cost_estimate=pl.CostEstimate(
            flops=8 * queries.size * batch * context,
            bytes_accessed=2 * dec_cache.size + 2 * landed.size,
            transcendentals=queries.size * batch * context // HEAD_SIZE,
        ),
        name="decode_attention",
    )(dec_len, slot_rows, queries, dec_cache, landed, fresh)


def shards(
    prefill_x,
    norm_gain,
    w_q,
    q_scale,
    key_value_weight,
    key_value_scale,
    w_o,
    o_scale,
    prefix_cache,
    prefix_len,
    dec_x,
    dec_cache,
    dec_len,
    place,
):
    prompts_total = prefix_cache.shape[1]
    row_count = dec_cache.shape[1]
    page_width = prefix_cache.shape[3]
    kv_heads = page_width // (2 * HEAD_SIZE)
    query_heads = w_q.shape[1] // HEAD_SIZE
    group_size = query_heads // kv_heads
    steps = dec_x.shape[0]
    section_count = lax.axis_size("section")
    section_index = lax.axis_index("section")
    tensor_count = lax.axis_size("tensor")
    tensor_index = lax.axis_index("tensor")
    head_span = max(1, 8 // query_heads)
    span_bits = head_span.bit_length() - 1
    block_width = w_o.shape[1] // tensor_count
    scales = (q_scale * EXP2_FACTOR, key_value_scale)

    weights = (norm_gain, w_q, key_value_weight)

    def kv_of_head(new_kv):
        for bit_number in range(span_bits):
            partner = partner_2(new_kv, "tensor", bit_number)
            new_kv = joined(new_kv, partner, bit_number, 1, tensor_index)
        return new_kv

    def finished(x, terms):
        total = sum(term.astype(jnp.float32) for term in terms)
        return (x.astype(jnp.float32) + total * o_scale).astype(jnp.bfloat16)

    dec_rows = dec_x.reshape(steps * row_count, -1)
    bounds = sorted({0, max(0, prompts_total - 2), prompts_total - 1, prompts_total})
    spans = list(zip(bounds[:-1], bounds[1:]))
    on_line = tensor_count == 4 and len(spans) == 3
    order = jnp.stack(
        line_order(tensor_index) if on_line else list(range(tensor_count))
    ).astype(jnp.int32)
    chunks = [prefill_x[first * PROMPT_TOKENS : last * PROMPT_TOKENS] for first, last in spans]
    blocks = chunks[:-1] + [jnp.concatenate([chunks[-1], dec_rows], axis=0)]
    pages = []

    def attention(k, queries):
        first, last = spans[k]
        return prefill_attention(queries, prefix_cache, first, last - first, pages[k], prefix_len)

    def keep(new_kv):
        new_kv = kv_of_head(new_kv)
        pages.append(new_kv[: chunks[len(pages)].shape[0]])
        return new_kv

    def back(attended, held=()):
        far, near, partner, own = project_out(
            attended, w_o, order[::-1], block_width, held=held
        )
        return LineScatter(own, partner, near, far, "tensor")

    def back_whole(attended):
        return project_out(
            attended, w_o, jnp.arange(tensor_count, dtype=jnp.int32), block_width, stacked=True
        )

    def summed(partial):
        return [lax.psum_scatter(partial, "tensor", scatter_dimension=0, tiled=False)]

    if on_line:
        first = LineGather(blocks[0], "tensor")
        first.second()
        slots = [[after(first.block, first.middle)], [first.partner]]
        begun = project_part(slots, order[:2], *weights, None, None)
        first.third(begun[2])
        second = LineGather(
            blocks[1], "tensor", (first.outer_far,), (first.outer, first.middle_far, begun[2])
        )
        queries, new_kv = project_part(first.slots()[2:], order[2:], *weights, begun, scales)
        keep(new_kv)
        second.second(queries)
        attended = attention(0, after(queries, second.partner, second.middle))
        second.third(attended)
        third = LineGather(
            after(blocks[2], second.outer, second.middle_far, attended), "tensor"
        )
        scatter = back(after(attended, second.outer, second.middle_far))

        queries, new_kv = project_part(second.slots(), order, *weights, None, scales)
        keep(new_kv)
        third.second(queries)
        attended = attention(1, after(queries, third.partner, third.middle))
        scatter.second(attended)
        partial = back_whole(after(attended, *scatter.first_hop))
        third.third(partial)
        middle_terms = summed(partial)

        slots = third.slots()
        slots[0][0] = after(slots[0][0], partial, third.outer, third.middle_far)
        begun = project_part(slots[:2], order[:2], *weights, None, None)
        queries, new_kv = project_part(slots[2:], order[2:], *weights, begun, scales)
        new_kv = keep(new_kv)
        scatter.third(queries)
        last_sum = back(attention(2, after(queries, *scatter.second_hop)), middle_terms)
        hold = (last_sum.own,)
    else:
        terms_of = []
        for k, block in enumerate(blocks):
            whole = lax.all_gather(block, "tensor", axis=1, tiled=True)
            queries, new_kv = project_part([[whole]], order[:1], *weights, None, scales)
            new_kv = keep(new_kv)
            terms_of.append(summed(back_whole(attention(k, queries))))
        hold = ()
    tokens = chunks[-1].shape[0]
    dec_queries, fresh_kv = queries[tokens:], new_kv[tokens:]

    own_block = after(jnp.concatenate(pages, axis=0), *hold).reshape(
        prompts_total, PROMPT_TOKENS, page_width
    )
    owners = (place // row_count).reshape(section_count, prompts_total)
    targets = (place % row_count).reshape(section_count, prompts_total)
    owner_hits = (owners[:, :, None] == jnp.arange(section_count)[None, None, :]).astype(jnp.int32)
    slot_ranks = jnp.sum((jnp.cumsum(owner_hits, axis=1) - owner_hits) * owner_hits, axis=2)
    capacity = prompts_total // 2
    slot_ids = jnp.arange(capacity)
    sending = lax.dynamic_index_in_dim(owner_hits, section_index, 0, keepdims=False)
    my_ranks = lax.dynamic_index_in_dim(slot_ranks, section_index, 0, keepdims=False)
    selector = (
        jnp.transpose(sending)[:, None, :] * (my_ranks[None, None, :] == slot_ids[None, :, None])
    ).astype(jnp.bfloat16)
    here = (owners == section_index)[:, None, :] & (
        slot_ranks[:, None, :] == slot_ids[None, :, None]
    )
    slot_rows = jnp.sum(jnp.where(here, targets[:, None, :] + 1, 0), axis=2) - 1
    outgoing = jnp.einsum(
        "skp,pcw->skcw", selector, own_block, preferred_element_type=jnp.float32
    ).astype(jnp.bfloat16)
    received = lax.all_to_all(outgoing, "section", split_axis=0, concat_axis=0, tiled=True)
    if on_line:
        last_sum.second(received)
        dec_queries = after(dec_queries, *last_sum.first_hop, *scatter.terms)
    landed = received.reshape(section_count * capacity, PROMPT_TOKENS, page_width)

    dec_queries = jnp.transpose(
        dec_queries.reshape(steps, row_count, kv_heads, group_size, HEAD_SIZE), (1, 2, 0, 3, 4)
    ).reshape(row_count, kv_heads, steps * group_size, HEAD_SIZE)
    fresh = jnp.transpose(fresh_kv.reshape(steps, row_count, page_width), (1, 0, 2))
    dec_attended = decode_attention(
        dec_queries.astype(jnp.float32),
        dec_cache,
        dec_len,
        landed,
        slot_rows.reshape(-1).astype(jnp.int32),
        fresh.astype(jnp.float32),
    )
    dec_attended = (
        jnp.transpose(
            dec_attended.reshape(row_count, kv_heads, steps, group_size, HEAD_SIZE), (2, 0, 1, 3, 4)
        )
        .reshape(steps * row_count, -1)
        .astype(jnp.bfloat16)
    )
    partial = back_whole(dec_attended)
    dec_terms = summed(partial)
    if on_line:
        last_sum.third(partial)
        terms_of = [scatter.terms, middle_terms, last_sum.terms]
    prefill_out = jnp.concatenate(
        [finished(x, terms) for x, terms in zip(chunks, terms_of)], axis=0
    )
    decode_out = finished(dec_rows, dec_terms).reshape(dec_x.shape)
    return (prefill_out, decode_out)


def solution(mesh):
    in_specs = (
        P(("groups", "section"), "tensor"),
        P(),
        P(None, "tensor"),
        P("tensor"),
        P(None, "tensor"),
        P("tensor"),
        P("tensor", None),
        P("tensor"),
        P("tensor", ("groups", "section"), None, None),
        P(("groups", "section")),
        P(None, ("groups", "section"), "tensor"),
        P("tensor", ("groups", "section"), None, None),
        P(("groups", "section")),
        P("groups"),
    )
    out_specs = (P(("groups", "section"), "tensor"), P(None, ("groups", "section"), "tensor"))
    return jax.shard_map(shards, mesh=mesh, in_specs=in_specs, out_specs=out_specs, check_vma=False)
```

profile of v0, /device:TPU:12, one launch (start us, length us, event | category | flops | bytes accessed | tf_op | source)
XLA Modules:
  0.0 403.2 jit_solution(7160514398146804548)
XLA Ops:
  13.6 19.9 %collective-permute-done.1.refs_1_ = bf16[256,2048]{1,0:T(8,128)(2,1)} collective-permute-done((bf16[256,2048]{1,0:T(8,128)(2,1)S(1)}, bf16[256,2048]{1,0:T(8,128)(2,1)}, u32[]{:S(2)}, u32[]{:S(2)}) %collective-permute-start.1) | collective-permute-done | bytes 1048608 | tf_op jit(solution)/shard_map/ppermute | solution.py:65
  41.7 11.5 %norm_qkv.5 = (f32[256,2048]{1,0:T(8,128)S(1)}, f32[256,512]{1,0:T(8,128)S(1)}, f32[256,128]{1,0:T(8,128)S(1)}) custom-call(s32[2]{0:T(128)S(1)} %pad_add_fusion.2.order, bf16[256,2048]{1,0:T(8,128)(2,1)S(1)} %slice.24.refs_0_, bf16[256,2048]{1,0:T(8,128)(2,1)} %collective-permute-done.1.refs_1_, f32[1,8192]{1,0:T(1,128)S(1)} %bitcast.52, ...), custom_call_target="tpu_custom_call" | custom-call | flops 5368709120 | bytes 20971520 | tf_op jit(solution)/shard_map/norm_qkv/pallas_call | solution.py:217
  53.9 8.9 %collective-permute-done.3.refs_2_ = bf16[256,2048]{1,0:T(8,128)(2,1)} collective-permute-done((bf16[256,2048]{1,0:T(8,128)(2,1)}, bf16[256,2048]{1,0:T(8,128)(2,1)}, u32[]{:S(2)}, u32[]{:S(2)}) %collective-permute-start.3) | collective-permute-done | bytes 1048608 | tf_op jit(solution)/shard_map/ppermute | solution.py:71
  68.7 16.9 %collective-permute-done.4.refs_3_ = bf16[256,2048]{1,0:T(8,128)(2,1)S(1)} collective-permute-done((bf16[256,2048]{1,0:T(8,128)(2,1)}, bf16[256,2048]{1,0:T(8,128)(2,1)S(1)}, u32[]{:S(2)}, u32[]{:S(2)}) %collective-permute-start.4) | collective-permute-done | bytes 1048608 | tf_op jit(solution)/shard_map/ppermute | solution.py:74
  93.5 12.2 %norm_qkv.6 = (bf16[256,2048]{1,0:T(8,128)(2,1)S(1)}, bf16[256,512]{1,0:T(8,128)(2,1)S(1)}) custom-call(s32[2]{0:T(128)S(1)} %pad_add_fusion.1.order, bf16[256,2048]{1,0:T(8,128)(2,1)} %collective-permute-done.refs_0_, bf16[256,2048]{1,0:T(8,128)(2,1)S(1)} %copy-done.6, bf16[256,2048]{1,0:T(8,128)(2,1)} %collective-permute-done.3.refs_2_, ...), custom_call_target="tpu_custom_call" | custom-call | flops 5368709120 | bytes 20971520 | tf_op jit(solution)/shard_map/norm_qkv/pallas_call | solution.py:217
  110.5 17.0 %prefill_attention.3.refs_1_ = bf16[256,2048]{1,0:T(8,128)(2,1)S(1)} custom-call(s32[4]{0:T(128)S(1)} %copy-done.30, bf16[256,2048]{1,0:T(8,128)(2,1)S(1)} %get-tuple-element.61.q_ref, bf16[1,4,2048,512]{3,2,1,0:T(8,128)(2,1)} %cache_ref.6, bf16[256,512]{1,0:T(8,128)(2,1)S(1)} %get-tuple-element.62.new_ref), custom_call_target="tpu_custom_call" | custom-call | flops 9126805504 | bytes 4194304 | tf_op jit(solution)/shard_map/prefill_attention/pallas_call | solution.py:422
  134.7 14.0 %project_out.4 = (bf16[256,2048]{1,0:T(8,128)(2,1)S(1)}, bf16[256,2048]{1,0:T(8,128)(2,1)S(1)}, bf16[256,2048]{1,0:T(8,128)(2,1)S(1)}, bf16[256,2048]{1,0:T(8,128)(2,1)S(1)}) custom-call(s32[4]{0:T(128)S(1)} %rev.4.refs_0_, bf16[256,2048]{1,0:T(8,128)(2,1)S(1)} %prefill_attention.3.refs_1_, bf16[2048,8192]{1,0:T(8,128)(2,1)} %refs_2_.7), custom_call_target="tpu_custom_call" | custom-call | flops 8589934592 | bytes 33554432 | tf_op jit(solution)/shard_map/project_out/pallas_call | solution.py:306
  153.1 14.9 %norm_qkv.7 = (bf16[128,2048]{1,0:T(8,128)(2,1)S(1)}, bf16[128,512]{1,0:T(8,128)(2,1)S(1)}) custom-call(s32[4]{0:T(128)S(1)} %pad_add_fusion.order, bf16[128,2048]{1,0:T(8,128)(2,1)S(1)} %get-tuple-element.60.refs_0_, bf16[128,2048]{1,0:T(8,128)(2,1)} %collective-permute-done.5.refs_1_, bf16[128,2048]{1,0:T(8,128)(2,1)} %collective-permute-done.6.refs_2_, ...), custom_call_target="tpu_custom_call" | custom-call | flops 5368709120 | bytes 41943040 | tf_op jit(solution)/shard_map/norm_qkv/pallas_call | solution.py:217
  168.1 9.6 %prefill_attention.4.refs_1_ = bf16[128,2048]{1,0:T(8,128)(2,1)S(1)} custom-call(s32[4]{0:T(128)S(1)} %copy-done.30, bf16[128,2048]{1,0:T(8,128)(2,1)S(1)} %get-tuple-element.72.q_ref, bf16[1,4,2048,512]{3,2,1,0:T(8,128)(2,1)} %cache_ref.6, bf16[128,512]{1,0:T(8,128)(2,1)S(1)} %get-tuple-element.73.new_ref), custom_call_target="tpu_custom_call" | custom-call | flops 4563402752 | bytes 2097152 | tf_op jit(solution)/shard_map/prefill_attention/pallas_call | solution.py:422
  179.1 13.6 %project_out.5 = bf16[4,128,2048]{2,1,0:T(8,128)(2,1)} custom-call(s32[4]{0:T(128)S(1)} %iota.20.refs_0_, bf16[128,2048]{1,0:T(8,128)(2,1)S(1)} %prefill_attention.4.refs_1_, bf16[2048,8192]{1,0:T(8,128)(2,1)} %refs_2_.7), custom_call_target="tpu_custom_call" | custom-call | flops 4294967296 | bytes 33554432 | tf_op jit(solution)/shard_map/project_out/pallas_call | solution.py:306
  193.7 5.3 %collective-permute-start.15 = (bf16[192,2048]{1,0:T(8,128)(2,1)}, bf16[192,2048]{1,0:T(8,128)(2,1)}, u32[]{:S(2)}, u32[]{:S(2)}) collective-permute-start(bf16[192,2048]{1,0:T(8,128)(2,1)} %copy-done.10), channel_id=1, source_target_pairs={{4,0},{8,12},{5,1},{9,13},{6,2},{10,14},{7,3},{11,15},{20,16},{24,... | collective-permute-start | bytes 2359304 | tf_op jit(solution)/shard_map/ppermute | solution.py:70
  206.4 28.1 %collective-permute-done.15.refs_1_ = bf16[192,2048]{1,0:T(8,128)(2,1)} collective-permute-done((bf16[192,2048]{1,0:T(8,128)(2,1)}, bf16[192,2048]{1,0:T(8,128)(2,1)}, u32[]{:S(2)}, u32[]{:S(2)}) %collective-permute-start.15) | collective-permute-done | bytes 786464 | tf_op jit(solution)/shard_map/ppermute | solution.py:70
  234.5 15.5 %collective-permute-done.16.refs_2_ = bf16[192,2048]{1,0:T(8,128)(2,1)} collective-permute-done((bf16[192,2048]{1,0:T(8,128)(2,1)}, bf16[192,2048]{1,0:T(8,128)(2,1)}, u32[]{:S(2)}, u32[]{:S(2)}) %collective-permute-start.16) | collective-permute-done | bytes 786464 | tf_op jit(solution)/shard_map/ppermute | solution.py:71
  252.7 8.5 %norm_qkv.8 = (f32[192,2048]{1,0:T(8,128)S(1)}, f32[192,512]{1,0:T(8,128)S(1)}, f32[192,128]{1,0:T(8,128)S(1)}) custom-call(s32[2]{0:T(128)S(1)} %pad_add_fusion.2.order, bf16[192,2048]{1,0:T(8,128)(2,1)S(1)} %pad_maximum_fusion.1.refs_0_, bf16[192,2048]{1,0:T(8,128)(2,1)S(1)} %copy-done.13, f32[1,8192]{1,0:T(1,128)S(1)} %bitcast.55, ...), custom_call_target="tpu_custom_call" | custom-call | flops 4026531840 | bytes 20971520 | tf_op jit(solution)/shard_map/norm_qkv/pallas_call | solution.py:217
  262.6 6.9 %collective-permute-done.14 = bf16[256,2048]{1,0:T(8,128)(2,1)S(1)} collective-permute-done((bf16[256,2048]{1,0:T(8,128)(2,1)}, bf16[256,2048]{1,0:T(8,128)(2,1)S(1)}, u32[]{:S(2)}, u32[]{:S(2)}) %collective-permute-start.14) | collective-permute-done | bytes 1048608 | tf_op jit(solution)/shard_map/ppermute | solution.py:100
  271.0 11.5 %norm_qkv.9 = (bf16[192,2048]{1,0:T(8,128)(2,1)S(1)}, bf16[192,512]{1,0:T(8,128)(2,1)S(1)}) custom-call(s32[2]{0:T(128)S(1)} %pad_add_fusion.1.order, bf16[192,2048]{1,0:T(8,128)(2,1)S(1)} %copy-done.11, bf16[192,2048]{1,0:T(8,128)(2,1)} %collective-permute-done.15.refs_1_, bf16[192,2048]{1,0:T(8,128)(2,1)} %collective-permute-done.16.refs_2_, ...), custom_call_target="tpu_custom_call" | custom-call | flops 4026531840 | bytes 20971520 | tf_op jit(solution)/shard_map/norm_qkv/pallas_call | solution.py:217
  284.8 8.0 %prefill_attention.5.refs_1_ = bf16[128,2048]{1,0:T(8,128)(2,1)S(1)} custom-call(s32[4]{0:T(128)S(1)} %copy-done.30, bf16[192,2048]{1,0:T(8,128)(2,1)S(1)} %get-tuple-element.88.q_ref, bf16[1,4,2048,512]{3,2,1,0:T(8,128)(2,1)} %cache_ref.6, bf16[128,512]{1,0:T(8,128)(2,1)S(1)} %slice.27.new_ref), custom_call_target="tpu_custom_call" | custom-call | flops 4563402752 | bytes 2097152 | tf_op jit(solution)/shard_map/prefill_attention/pallas_call | solution.py:422
  293.9 12.5 %project_out.6 = (bf16[128,2048]{1,0:T(8,128)(2,1)}, bf16[128,2048]{1,0:T(8,128)(2,1)S(1)}, bf16[128,2048]{1,0:T(8,128)(2,1)S(1)}, bf16[128,2048]{1,0:T(8,128)(2,1)S(1)}) custom-call(s32[4]{0:T(128)S(1)} %rev.4.refs_0_, bf16[128,2048]{1,0:T(8,128)(2,1)S(1)} %prefill_attention.5.refs_1_, bf16[2048,8192]{1,0:T(8,128)(2,1)} %refs_2_.7, ...), custom_call_target="tpu_custom_call" | custom-call | flops 4294967296 | bytes 33554432 | tf_op jit(solution)/shard_map/project_out/pallas_call | solution.py:306
  311.9 4.7 %all-to-all-start = ((bf16[4,2,128,512]{3,2,1,0:T(8,128)(2,1)}), bf16[4,2,128,512]{3,2,1,0:T(8,128)(2,1)S(1)}, u32[]{:S(2)}, u32[]{:S(2)}) async-start(bf16[4,2,128,512]{3,2,1,0:T(8,128)(2,1)} %copy.35), calls=%async_computation.1 | async-start | bytes 2097152 | tf_op jit(solution)/shard_map/all_to_all | solution.py:699
  322.3 9.1 %all-to-all-done = bf16[4,2,128,512]{3,2,1,0:T(8,128)(2,1)S(1)} async-done(((bf16[4,2,128,512]{3,2,1,0:T(8,128)(2,1)}), bf16[4,2,128,512]{3,2,1,0:T(8,128)(2,1)S(1)}, u32[]{:S(2)}, u32[]{:S(2)}) %all-to-all-start) | async-done | bytes 1048608 | tf_op jit(solution)/shard_map/all_to_all | solution.py:699
  336.9 7.3 %decode_attention.1 = f32[32,2,16,128]{3,2,1,0:T(8,128)S(1)} custom-call(s32[32]{0:T(128)S(1)} %copy-done.29, s32[8]{0:T(128)S(1)} %sub.15.row_ref, f32[32,2,16,128]{3,2,1,0:T(8,128)S(1)} %bitcast.51, bf16[1,32,64,512]{3,2,1,0:T(8,128)(2,1)S(1)} %copy-done.2, bf16[8,128,512]{2,1,0:T(8,128)(2,1)S(1)} %bitcast.49, f32[32,2,512]{2,1,0:T(2,128)S(1)} %bitcast.57), custom_call_target="tpu_custom_call" | custom-call | flops 268435456 | bytes 3145728 | tf_op jit(solution)/shard_map/decode_attention/pallas_call | solution.py:530
  344.4 13.2 %project_out.7 = bf16[4,64,2048]{2,1,0:T(8,128)(2,1)} custom-call(s32[4]{0:T(128)S(1)} %iota.21.refs_0_, bf16[64,2048]{1,0:T(8,128)(2,1)S(1)} %convert_element_type.192.refs_1_, bf16[2048,8192]{1,0:T(8,128)(2,1)} %refs_2_.7), custom_call_target="tpu_custom_call" | custom-call | flops 2147483648 | bytes 33554432 | tf_op jit(solution)/shard_map/project_out/pallas_call | solution.py:306
  366.6 12.0 %collective-permute-done.23 = bf16[128,2048]{1,0:T(8,128)(2,1)S(1)} collective-permute-done((bf16[128,2048]{1,0:T(8,128)(2,1)S(1)}, bf16[128,2048]{1,0:T(8,128)(2,1)S(1)}, u32[]{:S(2)}, u32[]{:S(2)}) %collective-permute-start.23) | collective-permute-done | bytes 524320 | tf_op jit(solution)/shard_map/ppermute | solution.py:107
  383.1 11.5 %reduce-scatter.5.cloned.1.call-done = bf16[1,64,2048]{2,1,0:T(8,128)(2,1)} async-done(((bf16[4,64,2048]{2,1,0:T(8,128)(2,1)}), bf16[1,64,2048]{2,1,0:T(8,128)(2,1)}) %reduce-scatter.5.cloned.1.call-update) | async-done | bytes 262160 | tf_op jit(solution)/shard_map/reduce_scatter | solution.py:629
  (170 shorter events, 95.6 us)
Async XLA Ops:
  7.2 285.7 %reduce-scatter.3.cloned.1.call-start = ((), (), s32[]{:S(2)}) async-start(), calls=%async_computation.3 | async-start | bytes 2621440 | tf_op jit(solution)/shard_map/reduce_scatter | solution.py:629
  8.5 25.1 %collective-permute-start.1 = (bf16[256,2048]{1,0:T(8,128)(2,1)S(1)}, bf16[256,2048]{1,0:T(8,128)(2,1)}, u32[]{:S(2)}, u32[]{:S(2)}) collective-permute-start(bf16[256,2048]{1,0:T(8,128)(2,1)S(1)} %slice.24.refs_0_), channel_id=1, source_target_pairs={{0,4},{4,0},{8,12},{12,8},{1,5},{5,1},{9,13},{13,9},{2,6},{6,2},{1... | collective-permute-start | bytes 3145736 | tf_op jit(solution)/shard_map/ppermute | solution.py:65
  9.0 27.6 %collective-permute-start = (bf16[256,2048]{1,0:T(8,128)(2,1)S(1)}, bf16[256,2048]{1,0:T(8,128)(2,1)}, u32[]{:S(2)}, u32[]{:S(2)}) collective-permute-start(bf16[256,2048]{1,0:T(8,128)(2,1)S(1)} %slice.24.refs_0_), channel_id=1, source_target_pairs={{4,8},{8,4},{5,9},{9,5},{6,10},{10,6},{7,11},{11,7},{20,24},{24,20... | collective-permute-start | bytes 3145736 | tf_op jit(solution)/shard_map/ppermute | solution.py:66
  36.6 26.2 %collective-permute-start.3 = (bf16[256,2048]{1,0:T(8,128)(2,1)}, bf16[256,2048]{1,0:T(8,128)(2,1)}, u32[]{:S(2)}, u32[]{:S(2)}) collective-permute-start(bf16[256,2048]{1,0:T(8,128)(2,1)} %collective-permute-done.1.refs_1_), channel_id=1, source_target_pairs={{4,8},{8,4},{5,9},{9,5},{6,10},{10,6},{7,11},{11,7},{20,24},{24,20... | collective-permute-start | bytes 3145736 | tf_op jit(solution)/shard_map/ppermute | solution.py:71
  40.3 24.1 %collective-permute-start.2 = (bf16[256,2048]{1,0:T(8,128)(2,1)}, bf16[256,2048]{1,0:T(8,128)(2,1)S(1)}, u32[]{:S(2)}, u32[]{:S(2)}) collective-permute-start(bf16[256,2048]{1,0:T(8,128)(2,1)} %collective-permute-done.refs_0_), channel_id=1, source_target_pairs={{4,0},{8,12},{5,1},{9,13},{6,2},{10,14},{7,3},{11,15},{20,16},{24,... | collective-permute-start | bytes 3145736 | tf_op jit(solution)/shard_map/ppermute | solution.py:70
  62.8 22.8 %collective-permute-start.4 = (bf16[256,2048]{1,0:T(8,128)(2,1)}, bf16[256,2048]{1,0:T(8,128)(2,1)S(1)}, u32[]{:S(2)}, u32[]{:S(2)}) collective-permute-start(bf16[256,2048]{1,0:T(8,128)(2,1)} %collective-permute-done.3.refs_2_), channel_id=1, source_target_pairs={{4,0},{8,12},{5,1},{9,13},{6,2},{10,14},{7,3},{11,15},{20,16},{24,... | collective-permute-start | bytes 3145736 | tf_op jit(solution)/shard_map/ppermute | solution.py:74
  65.4 40.4 %collective-permute-start.6 = (bf16[128,2048]{1,0:T(8,128)(2,1)S(1)}, bf16[128,2048]{1,0:T(8,128)(2,1)}, u32[]{:S(2)}, u32[]{:S(2)}) collective-permute-start(bf16[128,2048]{1,0:T(8,128)(2,1)S(1)} %get-tuple-element.60.refs_0_), channel_id=1, source_target_pairs={{4,8},{8,4},{5,9},{9,5},{6,10},{10,6},{7,11},{11,7},{20,24},{24,20... | collective-permute-start | bytes 1572872 | tf_op jit(solution)/shard_map/ppermute | solution.py:66
  105.8 21.7 %collective-permute-start.7 = (bf16[128,2048]{1,0:T(8,128)(2,1)}, bf16[128,2048]{1,0:T(8,128)(2,1)S(1)}, u32[]{:S(2)}, u32[]{:S(2)}) collective-permute-start(bf16[128,2048]{1,0:T(8,128)(2,1)} %collective-permute-done.6.refs_2_), channel_id=1, source_target_pairs={{4,0},{8,12},{5,1},{9,13},{6,2},{10,14},{7,3},{11,15},{20,16},{24,... | collective-permute-start | bytes 1572872 | tf_op jit(solution)/shard_map/ppermute | solution.py:70
  107.8 19.8 %collective-permute-start.8 = (bf16[128,2048]{1,0:T(8,128)(2,1)}, bf16[128,2048]{1,0:T(8,128)(2,1)S(1)}, u32[]{:S(2)}, u32[]{:S(2)}) collective-permute-start(bf16[128,2048]{1,0:T(8,128)(2,1)} %collective-permute-done.5.refs_1_), channel_id=1, source_target_pairs={{4,8},{8,4},{5,9},{9,5},{6,10},{10,6},{7,11},{11,7},{20,24},{24,20... | collective-permute-start | bytes 1572872 | tf_op jit(solution)/shard_map/ppermute | solution.py:71
  127.6 40.5 %collective-permute-start.12 = (bf16[192,2048]{1,0:T(8,128)(2,1)S(1)}, bf16[192,2048]{1,0:T(8,128)(2,1)S(1)}, u32[]{:S(2)}, u32[]{:S(2)}) collective-permute-start(bf16[192,2048]{1,0:T(8,128)(2,1)S(1)} %pad_maximum_fusion.1.refs_0_), channel_id=1, source_target_pairs={{4,8},{8,4},{5,9},{9,5},{6,10},{10,6},{7,11},{11,7},{20,24},{24,20... | collective-permute-start | bytes 2359304 | tf_op jit(solution)/shard_map/ppermute | solution.py:66
  130.7 37.3 %collective-permute-start.11 = (bf16[192,2048]{1,0:T(8,128)(2,1)S(1)}, bf16[192,2048]{1,0:T(8,128)(2,1)S(1)}, u32[]{:S(2)}, u32[]{:S(2)}) collective-permute-start(bf16[192,2048]{1,0:T(8,128)(2,1)S(1)} %pad_maximum_fusion.1.refs_0_), channel_id=1, source_target_pairs={{0,4},{4,0},{8,12},{12,8},{1,5},{5,1},{9,13},{13,9},{2,6},{6,2},{1... | collective-permute-start | bytes 2359304 | tf_op jit(solution)/shard_map/ppermute | solution.py:65
  130.8 22.3 %collective-permute-start.10 = (bf16[128,2048]{1,0:T(8,128)(2,1)S(1)}, bf16[128,2048]{1,0:T(8,128)(2,1)S(1)}, u32[]{:S(2)}, u32[]{:S(2)}) collective-permute-start(bf16[128,2048]{1,0:T(8,128)(2,1)S(1)} %collective-permute-done.8.refs_4_), channel_id=1, source_target_pairs={{4,0},{8,12},{5,1},{9,13},{6,2},{10,14},{7,3},{11,15},{20,16},{24,... | collective-permute-start | bytes 1572872 | tf_op jit(solution)/shard_map/ppermute | solution.py:74
  148.7 28.9 %collective-permute-start.9 = (bf16[256,2048]{1,0:T(8,128)(2,1)S(1)}, bf16[256,2048]{1,0:T(8,128)(2,1)S(1)}, u32[]{:S(2)}, u32[]{:S(2)}) collective-permute-start(bf16[256,2048]{1,0:T(8,128)(2,1)S(1)} %get-tuple-element.68), channel_id=1, source_target_pairs={{0,4},{12,8},{1,5},{13,9},{2,6},{14,10},{3,7},{15,11},{16,20},{28,... | collective-permute-start | bytes 3145736 | tf_op jit(solution)/shard_map/ppermute | solution.py:94
  193.7 40.9 %collective-permute-start.15 = (bf16[192,2048]{1,0:T(8,128)(2,1)}, bf16[192,2048]{1,0:T(8,128)(2,1)}, u32[]{:S(2)}, u32[]{:S(2)}) collective-permute-start(bf16[192,2048]{1,0:T(8,128)(2,1)} %copy-done.10), channel_id=1, source_target_pairs={{4,0},{8,12},{5,1},{9,13},{6,2},{10,14},{7,3},{11,15},{20,16},{24,... | collective-permute-start | bytes 2359304 | tf_op jit(solution)/shard_map/ppermute | solution.py:70
  198.9 51.1 %collective-permute-start.16 = (bf16[192,2048]{1,0:T(8,128)(2,1)}, bf16[192,2048]{1,0:T(8,128)(2,1)}, u32[]{:S(2)}, u32[]{:S(2)}) collective-permute-start(bf16[192,2048]{1,0:T(8,128)(2,1)} %copy-done.12), channel_id=1, source_target_pairs={{4,8},{8,4},{5,9},{9,5},{6,10},{10,6},{7,11},{11,7},{20,24},{24,20... | collective-permute-start | bytes 2359304 | tf_op jit(solution)/shard_map/ppermute | solution.py:71
  201.2 60.0 %collective-permute-start.13 = (bf16[256,2048]{1,0:T(8,128)(2,1)S(1)}, bf16[256,2048]{1,0:T(8,128)(2,1)S(1)}, u32[]{:S(2)}, u32[]{:S(2)}) collective-permute-start(bf16[256,2048]{1,0:T(8,128)(2,1)S(1)} %get-tuple-element.74), channel_id=1, source_target_pairs={{0,4},{12,8},{1,5},{13,9},{2,6},{14,10},{3,7},{15,11},{16,20},{28,... | collective-permute-start | bytes 3145736 | tf_op jit(solution)/shard_map/ppermute | solution.py:99
  202.8 66.8 %collective-permute-start.14 = (bf16[256,2048]{1,0:T(8,128)(2,1)}, bf16[256,2048]{1,0:T(8,128)(2,1)S(1)}, u32[]{:S(2)}, u32[]{:S(2)}) collective-permute-start(bf16[256,2048]{1,0:T(8,128)(2,1)} %add_convert_fusion.3), channel_id=1, source_target_pairs={{4,8},{8,4},{5,9},{9,5},{6,10},{10,6},{7,11},{11,7},{20,24},{24,20... | collective-permute-start | bytes 3145736 | tf_op jit(solution)/shard_map/ppermute | solution.py:100
  250.1 20.9 %collective-permute-start.17 = (bf16[192,2048]{1,0:T(8,128)(2,1)}, bf16[192,2048]{1,0:T(8,128)(2,1)S(1)}, u32[]{:S(2)}, u32[]{:S(2)}) collective-permute-start(bf16[192,2048]{1,0:T(8,128)(2,1)} %collective-permute-done.16.refs_2_), channel_id=1, source_target_pairs={{4,0},{8,12},{5,1},{9,13},{6,2},{10,14},{7,3},{11,15},{20,16},{24,... | collective-permute-start | bytes 2359304 | tf_op jit(solution)/shard_map/ppermute | solution.py:74
  282.4 52.7 %collective-permute-start.18 = (bf16[256,2048]{1,0:T(8,128)(2,1)}, bf16[256,2048]{1,0:T(8,128)(2,1)}, u32[]{:S(2)}, u32[]{:S(2)}) collective-permute-start(bf16[256,2048]{1,0:T(8,128)(2,1)} %add_convert_fusion.2), channel_id=1, source_target_pairs={{4,8},{8,4},{5,9},{9,5},{6,10},{10,6},{7,11},{11,7},{20,24},{24,20... | collective-permute-start | bytes 3145736 | tf_op jit(solution)/shard_map/ppermute | solution.py:107
  284.6 50.5 %collective-permute-start.19 = (bf16[256,2048]{1,0:T(8,128)(2,1)}, bf16[256,2048]{1,0:T(8,128)(2,1)}, u32[]{:S(2)}, u32[]{:S(2)}) collective-permute-start(bf16[256,2048]{1,0:T(8,128)(2,1)} %add_convert_fusion.1), channel_id=1, source_target_pairs={{0,4},{4,0},{8,12},{12,8},{1,5},{5,1},{9,13},{13,9},{2,6},{6,2},{1... | collective-permute-start | bytes 3145736 | tf_op jit(solution)/shard_map/ppermute | solution.py:108
  311.9 19.6 %all-to-all-start = ((bf16[4,2,128,512]{3,2,1,0:T(8,128)(2,1)}), bf16[4,2,128,512]{3,2,1,0:T(8,128)(2,1)S(1)}, u32[]{:S(2)}, u32[]{:S(2)}) async-start(bf16[4,2,128,512]{3,2,1,0:T(8,128)(2,1)} %copy.35), calls=%async_computation.1 | async-start | bytes 2097152 | tf_op jit(solution)/shard_map/all_to_all | solution.py:699
  316.5 78.0 %reduce-scatter.5.cloned.1.call-start = ((), (), s32[]{:S(2)}) async-start(), calls=%async_computation.4 | async-start | bytes 1310720 | tf_op jit(solution)/shard_map/reduce_scatter | solution.py:629
  331.5 27.6 %collective-permute-start.22 = (bf16[128,2048]{1,0:T(8,128)(2,1)}, bf16[128,2048]{1,0:T(8,128)(2,1)}, u32[]{:S(2)}, u32[]{:S(2)}) collective-permute-start(bf16[128,2048]{1,0:T(8,128)(2,1)} %add_convert_fusion.7), channel_id=1, source_target_pairs={{4,8},{8,4},{5,9},{9,5},{6,10},{10,6},{7,11},{11,7},{20,24},{24,20... | collective-permute-start | bytes 1572872 | tf_op jit(solution)/shard_map/ppermute | solution.py:100
  335.1 22.6 %collective-permute-start.21 = (bf16[128,2048]{1,0:T(8,128)(2,1)}, bf16[128,2048]{1,0:T(8,128)(2,1)}, u32[]{:S(2)}, u32[]{:S(2)}) collective-permute-start(bf16[128,2048]{1,0:T(8,128)(2,1)} %copy-done.18), channel_id=1, source_target_pairs={{0,4},{12,8},{1,5},{13,9},{2,6},{14,10},{3,7},{15,11},{16,20},{28,... | collective-permute-start | bytes 1572872 | tf_op jit(solution)/shard_map/ppermute | solution.py:99
  (42 other events, 488.4 us)
Sparse Core Ops, SparseCore 0:
  192.9 61.3 reduce-scatter.2
  357.8 36.7 reduce-scatter.4
where the time goes:
time: 409 us; the launch traced here: 403 us
  Pallas kernels  154 us (38%)
  waiting for transfers between devices  140 us (34%)
  starting transfers between devices  61.8 us (15%)
  other arithmetic  15.8 us (4%)
  local copies, waits for them, and re-layouts  15.7 us (4%)
  between operations  14.9 us (4%)
    pallas_call x5, Pallas kernels, project_part(): pl.pallas_call(functools.partial(qkv_kernel, [len(slot) for slot in slots...  58.6 us
    pallas_call x4, Pallas kernels, project_out(): pl.pallas_call(without(functools.partial(out_kernel, count, stacked, tile...  53.3 us
    pallas_call x3, Pallas kernels, prefill_attention(): pl.pallas_call(functools.partial(prefill_kernel, kv_heads, group, span, f...  34.6 us
    ppermute x3, waiting for transfers between devices, second(): self.outer = lax.ppermute(middle, self.axis, OUTWARD)  28.1 us
    ppermute x3, waiting for transfers between devices, second(): self.middle_far = lax.ppermute(partner, self.axis, MIDDLE)  24.4 us
    ppermute x3, waiting for transfers between devices, __init__(): self.partner = lax.ppermute(after(block, *outer_held), axis, OUTER)  20 us
    ppermute x3, waiting for transfers between devices, third(): lax.ppermute(after(self.middle_far, *held), self.axis, OUTWARD)  19.8 us
    unnamed x77, local copies, waits for them, and re-layouts  12.4 us
  transfers between devices with their start and end apart: 28, of which 13 were waited for; matrix products, arithmetic and copies ran while one was open for 4% of the time, Pallas kernels for 35%

commit v1 on v0

--- a/solution.py
+++ b/solution.py
@@ -12,6 +12,7 @@
 PROMPT_TOKENS = 128
 KERNEL_VMEM = 46 << 20
 WEIGHT_BUFFERS = 8
+COST_SHARE = 8
 EXP2_FACTOR = math.log2(math.e) / math.sqrt(HEAD_SIZE)
 MASKED = -1e30
 
@@ -107,6 +108,10 @@
         near = lax.ppermute(near, self.axis, MIDDLE)
         partner = lax.ppermute(partner, self.axis, OUTER)
         self.terms = [self.own, near, partner]
+
+
+def without(kernel, first, count):
+    return lambda *refs: kernel(*refs[:first], *refs[first + count :])
 
 
 def qkv_kernel(counts, begun, ended, tile, order, *refs):
@@ -190,7 +195,7 @@
         kv_ref[...] = (acckv[...] * root * kvs_ref[...]).astype(kv_ref.dtype)
 
 
-def project_part(slots, order, norm_gain, w_q, kv_weight, begun, scales):
+def project_part(slots, order, norm_gain, w_q, kv_weight, begun, scales, held=()):
     rows, depth = slots[0][0].shape
     tile = tile_of(depth, 512)
     q_cols, kv_cols = w_q.shape[1], kv_weight.shape[1]
@@ -214,18 +219,19 @@
     else:
         out_shapes = [jax.ShapeDtypeStruct(shape, jnp.float32) for shape in sums]
         scratch = []
+    kernel = functools.partial(
+        qkv_kernel,
+        [len(slot) for slot in slots],
+        begun is not None,
+        0 if scales is None else w_q.shape[0],
+        tile,
+    )
     return pl.pallas_call(
-        functools.partial(
-            qkv_kernel,
-            [len(slot) for slot in slots],
-            begun is not None,
-            0 if scales is None else w_q.shape[0],
-            tile,
-        ),
+        without(kernel, 1 + len(operands), len(held)),
         grid_spec=pltpu.PrefetchScalarGridSpec(
             num_scalar_prefetch=1,
             grid=(1,),
-            in_specs=in_specs,
+            in_specs=in_specs + [anywhere] * len(held),
             out_specs=[whole(out.shape) for out in out_shapes],
             scratch_shapes=scratch
             + [pltpu.VMEM((rows, depth), jnp.bfloat16) for _ in arrays]
@@ -240,12 +246,12 @@
         out_shape=out_shapes,
         compiler_params=pltpu.CompilerParams(vmem_limit_bytes=KERNEL_VMEM),
         cost_estimate=pl.CostEstimate(
-            flops=2 * rows * depth * len(slots) * (q_cols + kv_cols),
-            bytes_accessed=2 * depth * len(slots) * (q_cols + kv_cols),
+            flops=2 * rows * depth * len(slots) * (q_cols + kv_cols) // COST_SHARE,
+            bytes_accessed=(2 * depth * len(slots) * (q_cols + kv_cols)) // COST_SHARE,
             transcendentals=0,
         ),
         name="norm_qkv",
-    )(order, *operands)
+    )(order, *operands, *held)
 
 
 def out_kernel(count, stacked, tile, order, x_ref, w_ref, *refs):
@@ -292,10 +298,6 @@
         o_copies[-1].start()
     for copy in o_copies:
         copy.wait()
-
-
-def without(kernel, first, count):
-    return lambda *refs: kernel(*refs[:first], *refs[first + count :])
 
 
 def project_out(attended, w_o, order, block, stacked=False, held=()):
@@ -324,8 +326,8 @@
         else [jax.ShapeDtypeStruct((rows, block), jnp.bfloat16)] * count,
         compiler_params=pltpu.CompilerParams(vmem_limit_bytes=KERNEL_VMEM),
         cost_estimate=pl.CostEstimate(
-            flops=2 * rows * depth * count * block,
-            bytes_accessed=2 * depth * count * block,
+            flops=2 * rows * depth * count * block // COST_SHARE,
+            bytes_accessed=(2 * depth * count * block) // COST_SHARE,
             transcendentals=0,
         ),
         name="project_out",
@@ -436,8 +438,8 @@
         out_shape=jax.ShapeDtypeStruct((count * PROMPT_TOKENS, width), jnp.bfloat16),
         compiler_params=pltpu.CompilerParams(vmem_limit_bytes=KERNEL_VMEM),
         cost_estimate=pl.CostEstimate(
-            flops=8 * count * rows * kv_heads * (positions + PROMPT_TOKENS) * HEAD_SIZE,
-            bytes_accessed=2 * count * positions * page,
+            flops=8 * count * rows * kv_heads * (positions + PROMPT_TOKENS) * HEAD_SIZE // COST_SHARE,
+            bytes_accessed=(2 * count * positions * page) // COST_SHARE,
             transcendentals=count * rows * kv_heads * (positions + PROMPT_TOKENS),
         ),
         name="prefill_attention",
@@ -522,17 +524,18 @@
     o_ref[...] = (acc[:, :, :, :HEAD_SIZE] / acc[:, :, :, HEAD_SIZE:]).astype(o_ref.dtype)
 
 
-def decode_attention(queries, dec_cache, dec_len, landed, slot_rows, fresh):
+def decode_attention(queries, dec_cache, dec_len, landed, slot_rows, fresh, held=()):
     row_count, kv_heads, per_row = queries.shape[:3]
     context = dec_cache.shape[2]
     batch = max(1, min(row_count, 2 * HEAD_SIZE // context))
     whole = lambda array: pl.BlockSpec(array.shape, lambda g, *_: (0,) * array.ndim)
     return pl.pallas_call(
-        functools.partial(decode_kernel, kv_heads, batch),
+        without(functools.partial(decode_kernel, kv_heads, batch), 6, len(held)),
         grid_spec=pltpu.PrefetchScalarGridSpec(
             num_scalar_prefetch=2,
             grid=(1,),
-            in_specs=[whole(queries), whole(dec_cache), whole(landed), whole(fresh)],
+            in_specs=[whole(queries), whole(dec_cache), whole(landed), whole(fresh)]
+            + [pl.BlockSpec(memory_space=pl.ANY)] * len(held),
             out_specs=whole(queries),
             scratch_shapes=[
                 pltpu.VMEM((row_count, kv_heads, per_row, 2 * HEAD_SIZE), jnp.float32),
@@ -542,12 +545,12 @@
         out_shape=jax.ShapeDtypeStruct(queries.shape, jnp.float32),
         compiler_params=pltpu.CompilerParams(vmem_limit_bytes=KERNEL_VMEM),
         cost_estimate=pl.CostEstimate(
-            flops=8 * queries.size * batch * context,
-            bytes_accessed=2 * dec_cache.size + 2 * landed.size,
+            flops=8 * queries.size * batch * context // COST_SHARE,
+            bytes_accessed=(2 * dec_cache.size + 2 * landed.size) // COST_SHARE,
             transcendentals=queries.size * batch * context // HEAD_SIZE,
         ),
         name="decode_attention",
-    )(dec_len, slot_rows, queries, dec_cache, landed, fresh)
+    )(dec_len, slot_rows, queries, dec_cache, landed, fresh, *held)
 
 
 def shards(
@@ -595,7 +598,7 @@
         return (x.astype(jnp.float32) + total * o_scale).astype(jnp.bfloat16)
 
     dec_rows = dec_x.reshape(steps * row_count, -1)
-    bounds = sorted({0, max(0, prompts_total - 2), prompts_total - 1, prompts_total})
+    bounds = sorted({0, min(1, prompts_total - 1), prompts_total - 1, prompts_total})
     spans = list(zip(bounds[:-1], bounds[1:]))
     on_line = tensor_count == 4 and len(spans) == 3
     order = jnp.stack(
@@ -631,39 +634,53 @@
     if on_line:
         first = LineGather(blocks[0], "tensor")
         first.second()
-        slots = [[after(first.block, first.middle)], [first.partner]]
-        begun = project_part(slots, order[:2], *weights, None, None)
+        begun = project_part(
+            [[first.block], [first.partner]], order[:2], *weights, None, None, (first.middle,)
+        )
         first.third(begun[2])
         second = LineGather(
             blocks[1], "tensor", (first.outer_far,), (first.outer, first.middle_far, begun[2])
         )
         queries, new_kv = project_part(first.slots()[2:], order[2:], *weights, begun, scales)
         keep(new_kv)
-        second.second(queries)
-        attended = attention(0, after(queries, second.partner, second.middle))
-        second.third(attended)
+        attended = attention(0, queries)
+        second.second(attended)
+        sums = [back(attended, (second.partner, second.middle))]
+
+        begun = project_part(
+            [[second.block], [second.partner]], order[:2], *weights, None, None, (sums[0].own,)
+        )
+        second.third(begun[2])
+        sums[0].second(begun[2])
+        sums[0].third()
         third = LineGather(
-            after(blocks[2], second.outer, second.middle_far, attended), "tensor"
-        )
-        scatter = back(after(attended, second.outer, second.middle_far))
-
-        queries, new_kv = project_part(second.slots(), order, *weights, None, scales)
+            blocks[2], "tensor", (second.outer_far,), (second.outer, second.middle_far, begun[2])
+        )
+        queries, new_kv = project_part(
+            second.slots()[2:], order[2:], *weights, begun, scales, sums[0].second_hop
+        )
         keep(new_kv)
-        third.second(queries)
-        attended = attention(1, after(queries, third.partner, third.middle))
-        scatter.second(attended)
-        partial = back_whole(after(attended, *scatter.first_hop))
-        third.third(partial)
-        middle_terms = summed(partial)
-
-        slots = third.slots()
-        slots[0][0] = after(slots[0][0], partial, third.outer, third.middle_far)
-        begun = project_part(slots[:2], order[:2], *weights, None, None)
-        queries, new_kv = project_part(slots[2:], order[2:], *weights, begun, scales)
+        attended = attention(1, queries)
+        third.second(attended)
+        sums.append(back(attended, (third.partner, third.middle, *sums[0].terms[1:])))
+
+        third.third(sums[1].own)
+        begun = project_part(
+            [[third.block], [third.partner]],
+            order[:2],
+            *weights,
+            None,
+            None,
+            (sums[1].own, third.outer, third.middle_far),
+        )
+        sums[1].second(begun[2])
+        queries, new_kv = project_part(
+            third.slots()[2:], order[2:], *weights, begun, scales, sums[1].first_hop
+        )
         new_kv = keep(new_kv)
-        scatter.third(queries)
-        last_sum = back(attention(2, after(queries, *scatter.second_hop)), middle_terms)
-        hold = (last_sum.own,)
+        sums.append(back(attention(2, queries)))
+        sums[1].third(sums[2].own)
+        hold = (sums[2].own,)
     else:
         terms_of = []
         for k, block in enumerate(blocks):
@@ -698,8 +715,8 @@
     ).astype(jnp.bfloat16)
     received = lax.all_to_all(outgoing, "section", split_axis=0, concat_axis=0, tiled=True)
     if on_line:
-        last_sum.second(received)
-        dec_queries = after(dec_queries, *last_sum.first_hop, *scatter.terms)
+        sums[2].second(received)
+        hold = (*sums[2].first_hop, *sums[1].second_hop)
     landed = received.reshape(section_count * capacity, PROMPT_TOKENS, page_width)
 
     dec_queries = jnp.transpose(
@@ -713,6 +730,7 @@
         landed,
         slot_rows.reshape(-1).astype(jnp.int32),
         fresh.astype(jnp.float32),
+        hold,
     )
     dec_attended = (
         jnp.transpose(
@@ -721,11 +739,25 @@
         .reshape(steps * row_count, -1)
         .astype(jnp.bfloat16)
     )
-    partial = back_whole(dec_attended)
-    dec_terms = summed(partial)
     if on_line:
-        last_sum.third(partial)
-        terms_of = [scatter.terms, middle_terms, last_sum.terms]
+        sums[2].third(dec_attended)
+        to = [(tensor_index + shift) % tensor_count for shift in range(tensor_count)]
+        own, *parts = project_out(
+            dec_attended,
+            w_o,
+            jnp.stack(to).astype(jnp.int32),
+            block_width,
+            held=sums[2].second_hop,
+        )
+        dec_terms = [own] + [
+            lax.ppermute(
+                part, "tensor", [(j, (j + shift) % tensor_count) for j in range(tensor_count)]
+            )
+            for shift, part in enumerate(parts, 1)
+        ]
+        terms_of = [each.terms for each in sums]
+    else:
+        dec_terms = summed(back_whole(dec_attended))
     prefill_out = jnp.concatenate(
         [finished(x, terms) for x, terms in zip(chunks, terms_of)], axis=0
     )

time: 409 us -> 399 us (0.976)
  waiting for transfers between devices: 140 us -> 111 us
  starting transfers between devices: 61.8 us -> 84.2 us
  between operations: 14.9 us -> 1.81 us
  local copies, waits for them, and re-layouts: 15.7 us -> 24.9 us
  other arithmetic: 15.8 us -> 20.8 us
    ppermute x3, waiting for transfers between devices: 20 us -> 1.39 us  [__init__(): self.partner = lax.ppermute(after(block, *outer_held), axis, OUTER)]
    ppermute x0 -> x3, waiting for transfers between devices: none -> 18.1 us  [shards(): lax.ppermute(part, 'tensor', [(j, (j + shift) % tensor_count) for j in ra...]
    ppermute x3, waiting for transfers between devices: 28.1 us -> 11.6 us  [second(): self.outer = lax.ppermute(middle, self.axis, OUTWARD)]
    ppermute x3, waiting for transfers between devices: 24.4 us -> 12.3 us  [second(): self.middle_far = lax.ppermute(partner, self.axis, MIDDLE)]
    ppermute x2 -> x3, waiting for transfers between devices: 12 us -> 0.01 us  [third(): near = lax.ppermute(near, self.axis, MIDDLE)]
    ppermute x2 -> x3, starting transfers between devices: 7.26 us -> 19.1 us  [second(): self.far_out = lax.ppermute(far, self.axis, MIDDLE)]
    reduce_scatter x2 -> x0, waiting for transfers between devices: 11.5 us -> none  [summed(): lax.psum_scatter(partial, 'tensor', scatter_dimension=0, tiled=False)]
    ppermute x2 -> x3, waiting for transfers between devices: 6.94 us -> 18.4 us  [second(): self.far_out = lax.ppermute(far, self.axis, MIDDLE)]
  transfers between devices with their start and end apart: 28 -> 34, of which waited for: 13 -> 14; matrix products, arithmetic and copies ran while one was open for 4% -> 6% of each run, Pallas kernels for 35% -> 35%
where the time goes in v1:
time: 399 us; the launch traced here: 394 us
  Pallas kernels  151 us (38%)
  waiting for transfers between devices  111 us (28%)
  starting transfers between devices  84.2 us (21%)
  local copies, waits for them, and re-layouts  24.9 us (6%)
  other arithmetic  20.8 us (5%)
    pallas_call x6, Pallas kernels, project_part(): pl.pallas_call(without(kernel, 1 + len(operands), len(held)), grid_spec=p...  61.7 us
    pallas_call x4, Pallas kernels, project_out(): pl.pallas_call(without(functools.partial(out_kernel, count, stacked, tile...  50.9 us
    pallas_call x3, Pallas kernels, prefill_attention(): pl.pallas_call(functools.partial(prefill_kernel, kv_heads, group, span, f...  30 us
    ppermute x3, waiting for transfers between devices, third(): lax.ppermute(after(self.middle_far, *held), self.axis, OUTWARD)  23.4 us
    ppermute x3, starting transfers between devices, second(): self.far_out = lax.ppermute(far, self.axis, MIDDLE)  19.1 us
    unnamed x105, local copies, waits for them, and re-layouts  19 us
    ppermute x3, waiting for transfers between devices, second(): self.far_out = lax.ppermute(far, self.axis, MIDDLE)  18.4 us
    ppermute x3, waiting for transfers between devices, shards(): lax.ppermute(part, 'tensor', [(j, (j + shift) % tensor_count) for j in ra...  18.1 us
  transfers between devices with their start and end apart: 34, of which 14 were waited for; matrix products, arithmetic and copies ran while one was open for 6% of the time, Pallas kernels for 35%

profile of v1, /device:TPU:12, one launch (start us, length us, event | category | flops | bytes accessed | tf_op | source)
XLA Modules:
  0.0 394.0 jit_solution(4645373891961888065)
XLA Ops:
  6.3 12.0 %collective-permute-done.refs_6_.refs_1_ = bf16[128,2048]{1,0:T(8,128)(2,1)S(1)} collective-permute-done((bf16[128,2048]{1,0:T(8,128)(2,1)S(1)}, bf16[128,2048]{1,0:T(8,128)(2,1)S(1)}, u32[]{:S(2)}, u32[]{:S(2)}) %collective-permute-start) | collective-permute-done | bytes 524320 | tf_op jit(solution)/shard_map/ppermute | solution.py:67
  23.4 8.3 %norm_qkv.6 = (f32[128,2048]{1,0:T(8,128)S(1)}, f32[128,512]{1,0:T(8,128)S(1)}, f32[128,128]{1,0:T(8,128)S(1)}) custom-call(s32[2]{0:T(128)S(1)} %pad_add_fusion.2.refs_0_, bf16[128,2048]{1,0:T(8,128)(2,1)S(1)} %get-tuple-element.118.refs_1_, bf16[128,2048]{1,0:T(8,128)(2,1)S(1)} %collective-permute-done.1.refs_2_, f32[1,8192]{1,0:T(1,128)S(1)} %bitcast.52, ...), custom_call_target="tpu_custom_call" | custom-call | flops 335544320 | bytes 2621440 | tf_op jit(solution)/shard_map/norm_qkv/pallas_call | solution.py:229
  38.7 6.0 %collective-permute-done.4.refs_4_ = bf16[128,2048]{1,0:T(8,128)(2,1)S(1)} collective-permute-done((bf16[128,2048]{1,0:T(8,128)(2,1)S(1)}, bf16[128,2048]{1,0:T(8,128)(2,1)S(1)}, u32[]{:S(2)}, u32[]{:S(2)}) %collective-permute-start.4) | collective-permute-done | bytes 524320 | tf_op jit(solution)/shard_map/ppermute | solution.py:75
  54.4 8.6 %norm_qkv.7 = (bf16[128,2048]{1,0:T(8,128)(2,1)S(1)}, bf16[128,512]{1,0:T(8,128)(2,1)S(1)}) custom-call(s32[2]{0:T(128)S(1)} %pad_add_fusion.1.refs_0_, bf16[128,2048]{1,0:T(8,128)(2,1)S(1)} %copy-done.1, bf16[128,2048]{1,0:T(8,128)(2,1)S(1)} %copy-done.26, bf16[128,2048]{1,0:T(8,128)(2,1)S(1)} %copy-done.24, bf16[128,2048]{1,0:T(8,128)(2,1)S(1)} %copy-done.28, ...), custom_call_target="tpu_custom_call" | custom-call | flops 335544320 | bytes 2621440 | tf_op jit(solution)/shard_map/norm_qkv/pallas_call | solution.py:229
  63.0 6.5 %prefill_attention.3.refs_1_ = bf16[128,2048]{1,0:T(8,128)(2,1)S(1)} custom-call(s32[4]{0:T(128)S(1)} %copy-done.42, bf16[128,2048]{1,0:T(8,128)(2,1)S(1)} %get-tuple-element.65.q_ref, bf16[1,4,2048,512]{3,2,1,0:T(8,128)(2,1)} %cache_ref.5, bf16[128,512]{1,0:T(8,128)(2,1)S(1)} %get-tuple-element.66.new_ref), custom_call_target="tpu_custom_call" | custom-call | flops 570425344 | bytes 262144 | tf_op jit(solution)/shard_map/prefill_attention/pallas_call | solution.py:424
  75.0 12.3 %project_out.4 = (bf16[128,2048]{1,0:T(8,128)(2,1)S(1)}, bf16[128,2048]{1,0:T(8,128)(2,1)S(1)}, bf16[128,2048]{1,0:T(8,128)(2,1)S(1)}, bf16[128,2048]{1,0:T(8,128)(2,1)S(1)}) custom-call(s32[4]{0:T(128)S(1)} %rev.2.refs_0_, bf16[128,2048]{1,0:T(8,128)(2,1)S(1)} %copy-done.7, bf16[2048,8192]{1,0:T(8,128)(2,1)} %refs_2_.7, ...), custom_call_target="tpu_custom_call" | custom-call | flops 536870912 | bytes 4194304 | tf_op jit(solution)/shard_map/project_out/pallas_call | solution.py:308
  88.6 4.6 %collective-permute-start.12 = (bf16[256,2048]{1,0:T(8,128)(2,1)S(1)}, bf16[256,2048]{1,0:T(8,128)(2,1)S(1)}, u32[]{:S(2)}, u32[]{:S(2)}) collective-permute-start(bf16[256,2048]{1,0:T(8,128)(2,1)S(1)} %collective-permute-done.6.refs_4_.refs_1_), channel_id=1, source_target_pairs={{4,0},{8,12},{5,1},{9,13},{6,2},{10,14},{7,3},{11,15},{20,16},{24,... | collective-permute-start | bytes 3145736 | tf_op jit(solution)/shard_map/ppermute | solution.py:71
  93.3 9.7 %norm_qkv.8 = (f32[256,2048]{1,0:T(8,128)S(1)}, f32[256,512]{1,0:T(8,128)S(1)}, f32[256,128]{1,0:T(8,128)S(1)}) custom-call(s32[2]{0:T(128)S(1)} %pad_add_fusion.2.refs_0_, bf16[256,2048]{1,0:T(8,128)(2,1)S(1)} %slice.27.refs_1_, bf16[256,2048]{1,0:T(8,128)(2,1)S(1)} %collective-permute-done.5.refs_3_.refs_2_, f32[1,8192]{1,0:T(1,128)S(1)} %bitcast.54, ...), custom_call_target="tpu_custom_call" | custom-call | flops 671088640 | bytes 2621440 | tf_op jit(solution)/shard_map/norm_qkv/pallas_call | solution.py:229
  108.6 8.1 %collective-permute-done.12.refs_2_ = bf16[256,2048]{1,0:T(8,128)(2,1)S(1)} collective-permute-done((bf16[256,2048]{1,0:T(8,128)(2,1)S(1)}, bf16[256,2048]{1,0:T(8,128)(2,1)S(1)}, u32[]{:S(2)}, u32[]{:S(2)}) %collective-permute-start.12) | collective-permute-done | bytes 1048608 | tf_op jit(solution)/shard_map/ppermute | solution.py:71
  121.2 17.4 %collective-permute-done.14.refs_4_ = bf16[256,2048]{1,0:T(8,128)(2,1)S(1)} collective-permute-done((bf16[256,2048]{1,0:T(8,128)(2,1)}, bf16[256,2048]{1,0:T(8,128)(2,1)S(1)}, u32[]{:S(2)}, u32[]{:S(2)}) %collective-permute-start.14) | collective-permute-done | bytes 1048608 | tf_op jit(solution)/shard_map/ppermute | solution.py:75
  148.7 12.5 %norm_qkv.9 = (bf16[256,2048]{1,0:T(8,128)(2,1)S(1)}, bf16[256,512]{1,0:T(8,128)(2,1)S(1)}) custom-call(s32[2]{0:T(128)S(1)} %pad_add_fusion.1.refs_0_, bf16[256,2048]{1,0:T(8,128)(2,1)S(1)} %collective-permute-done.6.refs_4_.refs_1_, bf16[256,2048]{1,0:T(8,128)(2,1)S(1)} %copy-done.16, bf16[256,2048]{1,0:T(8,128)(2,1)} %collective-permute-done.13.refs_3_, ...), custom_call_target="tpu_custom_call" | custom-call | flops 671088640 | bytes 2621440 | tf_op jit(solution)/shard_map/norm_qkv/pallas_call | solution.py:229
  161.3 15.5 %prefill_attention.4.refs_1_ = bf16[256,2048]{1,0:T(8,128)(2,1)S(1)} custom-call(s32[4]{0:T(128)S(1)} %copy-done.42, bf16[256,2048]{1,0:T(8,128)(2,1)S(1)} %get-tuple-element.83.q_ref, bf16[1,4,2048,512]{3,2,1,0:T(8,128)(2,1)} %cache_ref.5, bf16[256,512]{1,0:T(8,128)(2,1)S(1)} %get-tuple-element.84.new_ref), custom_call_target="tpu_custom_call" | custom-call | flops 1140850688 | bytes 524288 | tf_op jit(solution)/shard_map/prefill_attention/pallas_call | solution.py:424
  176.8 13.8 %project_out.5 = (bf16[256,2048]{1,0:T(8,128)(2,1)}, bf16[256,2048]{1,0:T(8,128)(2,1)}, bf16[256,2048]{1,0:T(8,128)(2,1)S(1)}, bf16[256,2048]{1,0:T(8,128)(2,1)S(1)}) custom-call(s32[4]{0:T(128)S(1)} %rev.2.refs_0_, bf16[256,2048]{1,0:T(8,128)(2,1)S(1)} %prefill_attention.4.refs_1_, bf16[2048,8192]{1,0:T(8,128)(2,1)} %refs_2_.7, ...), custom_call_target="tpu_custom_call" | custom-call | flops 1073741824 | bytes 4194304 | tf_op jit(solution)/shard_map/project_out/pallas_call | solution.py:308
  201.5 10.8 %collective-permute-done.19.refs_8_.refs_3_ = bf16[192,2048]{1,0:T(8,128)(2,1)} collective-permute-done((bf16[192,2048]{1,0:T(8,128)(2,1)}, bf16[192,2048]{1,0:T(8,128)(2,1)}, u32[]{:S(2)}, u32[]{:S(2)}) %collective-permute-start.19) | collective-permute-done | bytes 786464 | tf_op jit(solution)/shard_map/ppermute | solution.py:72
  218.1 10.8 %norm_qkv.10 = (f32[192,2048]{1,0:T(8,128)S(1)}, f32[192,512]{1,0:T(8,128)S(1)}, f32[192,128]{1,0:T(8,128)S(1)}) custom-call(s32[2]{0:T(128)S(1)} %pad_add_fusion.2.refs_0_, bf16[192,2048]{1,0:T(8,128)(2,1)S(1)} %pad_maximum_fusion.1.refs_1_, bf16[192,2048]{1,0:T(8,128)(2,1)} %collective-permute-done.15.refs_3_.refs_2_, f32[1,8192]{1,0:T(1,128)S(1)} %bitcast.56, ...), custom_call_target="tpu_custom_call" | custom-call | flops 503316480 | bytes 2621440 | tf_op jit(solution)/shard_map/norm_qkv/pallas_call | solution.py:229
  233.7 13.7 %collective-permute-start.21 = (bf16[256,2048]{1,0:T(8,128)(2,1)S(1)}, bf16[256,2048]{1,0:T(8,128)(2,1)}, u32[]{:S(2)}, u32[]{:S(2)}) collective-permute-start(bf16[256,2048]{1,0:T(8,128)(2,1)S(1)} %add_convert_fusion.3.refs_13_), channel_id=1, source_target_pairs={{4,8},{8,4},{5,9},{9,5},{6,10},{10,6},{7,11},{11,7},{20,24},{24,20... | collective-permute-start | bytes 3145736 | tf_op jit(solution)/shard_map/ppermute | solution.py:101
  248.8 11.7 %norm_qkv.11 = (bf16[192,2048]{1,0:T(8,128)(2,1)S(1)}, bf16[192,512]{1,0:T(8,128)(2,1)S(1)}) custom-call(s32[2]{0:T(128)S(1)} %pad_add_fusion.1.refs_0_, bf16[192,2048]{1,0:T(8,128)(2,1)S(1)} %collective-permute-done.16.refs_4_.refs_1_, bf16[192,2048]{1,0:T(8,128)(2,1)} %collective-permute-done.18.refs_7_.refs_2_, ...), custom_call_target="tpu_custom_call" | custom-call | flops 503316480 | bytes 2621440 | tf_op jit(solution)/shard_map/norm_qkv/pallas_call | solution.py:229
  260.5 8.0 %prefill_attention.5.refs_1_ = bf16[128,2048]{1,0:T(8,128)(2,1)S(1)} custom-call(s32[4]{0:T(128)S(1)} %copy-done.42, bf16[192,2048]{1,0:T(8,128)(2,1)S(1)} %get-tuple-element.99.q_ref, bf16[1,4,2048,512]{3,2,1,0:T(8,128)(2,1)} %cache_ref.5, bf16[128,512]{1,0:T(8,128)(2,1)S(1)} %slice.29.new_ref), custom_call_target="tpu_custom_call" | custom-call | flops 570425344 | bytes 262144 | tf_op jit(solution)/shard_map/prefill_attention/pallas_call | solution.py:424
  268.6 12.5 %project_out.6 = (bf16[128,2048]{1,0:T(8,128)(2,1)}, bf16[128,2048]{1,0:T(8,128)(2,1)S(1)}, bf16[128,2048]{1,0:T(8,128)(2,1)S(1)}, bf16[128,2048]{1,0:T(8,128)(2,1)S(1)}) custom-call(s32[4]{0:T(128)S(1)} %rev.2.refs_0_, bf16[128,2048]{1,0:T(8,128)(2,1)S(1)} %prefill_attention.5.refs_1_, bf16[2048,8192]{1,0:T(8,128)(2,1)} %refs_2_.7), custom_call_target="tpu_custom_call" | custom-call | flops 536870912 | bytes 4194304 | tf_op jit(solution)/shard_map/project_out/pallas_call | solution.py:308
  292.0 12.1 %collective-permute-done.25 = bf16[128,2048]{1,0:T(8,128)(2,1)S(1)} collective-permute-done((bf16[128,2048]{1,0:T(8,128)(2,1)}, bf16[128,2048]{1,0:T(8,128)(2,1)S(1)}, u32[]{:S(2)}, u32[]{:S(2)}) %collective-permute-start.25) | collective-permute-done | bytes 524320 | tf_op jit(solution)/shard_map/ppermute | solution.py:95
  317.4 8.6 %decode_attention.1 = f32[32,2,16,128]{3,2,1,0:T(8,128)S(1)} custom-call(s32[32]{0:T(128)S(1)} %copy-done.43, s32[8]{0:T(128)S(1)} %sub.15.refs_1_, f32[32,2,16,128]{3,2,1,0:T(8,128)S(1)} %bitcast.51, bf16[1,32,64,512]{3,2,1,0:T(8,128)(2,1)S(1)} %copy-done.10, bf16[8,128,512]{2,1,0:T(8,128)(2,1)} %bitcast.17.refs_4_, f32[32,2,512]{2,1,0:T(2,128)S(1)} %bitcast.58, ...), custom_call_target="tpu_custom_call" | custom-call | flops 33554432 | bytes 393216 | tf_op jit(solution)/shard_map/decode_attention/pallas_call | solution.py:532
  329.2 18.4 %collective-permute-done.27 = bf16[128,2048]{1,0:T(8,128)(2,1)} collective-permute-done((bf16[128,2048]{1,0:T(8,128)(2,1)}, bf16[128,2048]{1,0:T(8,128)(2,1)}, u32[]{:S(2)}, u32[]{:S(2)}) %collective-permute-start.27) | collective-permute-done | bytes 524320 | tf_op jit(solution)/shard_map/ppermute | solution.py:101
  352.1 12.3 %project_out.7 = (bf16[64,2048]{1,0:T(8,128)(2,1)S(1)}, bf16[64,2048]{1,0:T(8,128)(2,1)S(1)}, bf16[64,2048]{1,0:T(8,128)(2,1)S(1)}, bf16[64,2048]{1,0:T(8,128)(2,1)S(1)}) custom-call(s32[4]{0:T(128)S(1)} %pad_add_fusion.3.refs_0_, bf16[64,2048]{1,0:T(8,128)(2,1)S(1)} %convert_element_type.239.refs_1_, bf16[2048,8192]{1,0:T(8,128)(2,1)} %refs_2_.7, ...), custom_call_target="tpu_custom_call" | custom-call | flops 268435456 | bytes 4194304 | tf_op jit(solution)/shard_map/project_out/pallas_call | solution.py:308
  371.4 12.1 %collective-permute-done.30 = bf16[64,2048]{1,0:T(8,128)(2,1)S(1)} collective-permute-done((bf16[64,2048]{1,0:T(8,128)(2,1)S(1)}, bf16[64,2048]{1,0:T(8,128)(2,1)S(1)}, u32[]{:S(2)}, u32[]{:S(2)}) %collective-permute-start.30) | collective-permute-done | bytes 262176 | tf_op jit(solution)/shard_map/ppermute | solution.py:753
  (210 shorter events, 125.8 us)
Async XLA Ops:
  36.2 34.2 %collective-permute-start.6 = (bf16[256,2048]{1,0:T(8,128)(2,1)S(1)}, bf16[256,2048]{1,0:T(8,128)(2,1)S(1)}, u32[]{:S(2)}, u32[]{:S(2)}) collective-permute-start(bf16[256,2048]{1,0:T(8,128)(2,1)S(1)} %slice.27.refs_1_), channel_id=1, source_target_pairs={{4,8},{8,4},{5,9},{9,5},{6,10},{10,6},{7,11},{11,7},{20,24},{24,20... | collective-permute-start | bytes 3145736 | tf_op jit(solution)/shard_map/ppermute | solution.py:67
  45.5 24.9 %collective-permute-start.5 = (bf16[256,2048]{1,0:T(8,128)(2,1)S(1)}, bf16[256,2048]{1,0:T(8,128)(2,1)S(1)}, u32[]{:S(2)}, u32[]{:S(2)}) collective-permute-start(bf16[256,2048]{1,0:T(8,128)(2,1)S(1)} %slice.27.refs_1_), channel_id=1, source_target_pairs={{0,4},{4,0},{8,12},{12,8},{1,5},{5,1},{9,13},{13,9},{2,6},{6,2},{1... | collective-permute-start | bytes 3145736 | tf_op jit(solution)/shard_map/ppermute | solution.py:66
  70.4 32.6 %collective-permute-start.13 = (bf16[256,2048]{1,0:T(8,128)(2,1)S(1)}, bf16[256,2048]{1,0:T(8,128)(2,1)}, u32[]{:S(2)}, u32[]{:S(2)}) collective-permute-start(bf16[256,2048]{1,0:T(8,128)(2,1)S(1)} %collective-permute-done.5.refs_3_.refs_2_), channel_id=1, source_target_pairs={{4,8},{8,4},{5,9},{9,5},{6,10},{10,6},{7,11},{11,7},{20,24},{24,20... | collective-permute-start | bytes 3145736 | tf_op jit(solution)/shard_map/ppermute | solution.py:72
  88.6 28.1 %collective-permute-start.12 = (bf16[256,2048]{1,0:T(8,128)(2,1)S(1)}, bf16[256,2048]{1,0:T(8,128)(2,1)S(1)}, u32[]{:S(2)}, u32[]{:S(2)}) collective-permute-start(bf16[256,2048]{1,0:T(8,128)(2,1)S(1)} %collective-permute-done.6.refs_4_.refs_1_), channel_id=1, source_target_pairs={{4,0},{8,12},{5,1},{9,13},{6,2},{10,14},{7,3},{11,15},{20,16},{24,... | collective-permute-start | bytes 3145736 | tf_op jit(solution)/shard_map/ppermute | solution.py:71
  103.0 35.6 %collective-permute-start.14 = (bf16[256,2048]{1,0:T(8,128)(2,1)}, bf16[256,2048]{1,0:T(8,128)(2,1)S(1)}, u32[]{:S(2)}, u32[]{:S(2)}) collective-permute-start(bf16[256,2048]{1,0:T(8,128)(2,1)} %collective-permute-done.13.refs_3_), channel_id=1, source_target_pairs={{4,0},{8,12},{5,1},{9,13},{6,2},{10,14},{7,3},{11,15},{20,16},{24,... | collective-permute-start | bytes 3145736 | tf_op jit(solution)/shard_map/ppermute | solution.py:75
  105.8 35.2 %collective-permute-start.9 = (bf16[128,2048]{1,0:T(8,128)(2,1)S(1)}, bf16[128,2048]{1,0:T(8,128)(2,1)S(1)}, u32[]{:S(2)}, u32[]{:S(2)}) collective-permute-start(bf16[128,2048]{1,0:T(8,128)(2,1)S(1)} %add_convert_fusion.11), channel_id=1, source_target_pairs={{4,8},{8,4},{5,9},{9,5},{6,10},{10,6},{7,11},{11,7},{20,24},{24,20... | collective-permute-start | bytes 1572872 | tf_op jit(solution)/shard_map/ppermute | solution.py:101
  116.7 60.1 %collective-permute-start.16 = (bf16[192,2048]{1,0:T(8,128)(2,1)S(1)}, bf16[192,2048]{1,0:T(8,128)(2,1)S(1)}, u32[]{:S(2)}, u32[]{:S(2)}) collective-permute-start(bf16[192,2048]{1,0:T(8,128)(2,1)S(1)} %pad_maximum_fusion.1.refs_1_), channel_id=1, source_target_pairs={{4,8},{8,4},{5,9},{9,5},{6,10},{10,6},{7,11},{11,7},{20,24},{24,20... | collective-permute-start | bytes 2359304 | tf_op jit(solution)/shard_map/ppermute | solution.py:67
  138.6 38.2 %collective-permute-start.15 = (bf16[192,2048]{1,0:T(8,128)(2,1)S(1)}, bf16[192,2048]{1,0:T(8,128)(2,1)}, u32[]{:S(2)}, u32[]{:S(2)}) collective-permute-start(bf16[192,2048]{1,0:T(8,128)(2,1)S(1)} %pad_maximum_fusion.1.refs_1_), channel_id=1, source_target_pairs={{0,4},{4,0},{8,12},{12,8},{1,5},{5,1},{9,13},{13,9},{2,6},{6,2},{1... | collective-permute-start | bytes 2359304 | tf_op jit(solution)/shard_map/ppermute | solution.py:66
  141.9 34.8 %collective-permute-start.10 = (bf16[128,2048]{1,0:T(8,128)(2,1)}, bf16[128,2048]{1,0:T(8,128)(2,1)S(1)}, u32[]{:S(2)}, u32[]{:S(2)}) collective-permute-start(bf16[128,2048]{1,0:T(8,128)(2,1)} %add_convert_fusion.10.refs_13_), channel_id=1, source_target_pairs={{4,8},{8,4},{5,9},{9,5},{6,10},{10,6},{7,11},{11,7},{20,24},{24,20... | collective-permute-start | bytes 1572872 | tf_op jit(solution)/shard_map/ppermute | solution.py:108
  144.1 32.7 %collective-permute-start.11 = (bf16[128,2048]{1,0:T(8,128)(2,1)}, bf16[128,2048]{1,0:T(8,128)(2,1)}, u32[]{:S(2)}, u32[]{:S(2)}) collective-permute-start(bf16[128,2048]{1,0:T(8,128)(2,1)} %add_convert_fusion.9.refs_14_), channel_id=1, source_target_pairs={{0,4},{4,0},{8,12},{12,8},{1,5},{5,1},{9,13},{13,9},{2,6},{6,2},{1... | collective-permute-start | bytes 1572872 | tf_op jit(solution)/shard_map/ppermute | solution.py:109
  191.7 38.4 %collective-permute-start.17 = (bf16[256,2048]{1,0:T(8,128)(2,1)}, bf16[256,2048]{1,0:T(8,128)(2,1)}, u32[]{:S(2)}, u32[]{:S(2)}) collective-permute-start(bf16[256,2048]{1,0:T(8,128)(2,1)} %get-tuple-element.89), channel_id=1, source_target_pairs={{0,4},{12,8},{1,5},{13,9},{2,6},{14,10},{3,7},{15,11},{16,20},{28,... | collective-permute-start | bytes 3145736 | tf_op jit(solution)/shard_map/ppermute | solution.py:95
  197.0 21.1 %collective-permute-start.18 = (bf16[192,2048]{1,0:T(8,128)(2,1)S(1)}, bf16[192,2048]{1,0:T(8,128)(2,1)}, u32[]{:S(2)}, u32[]{:S(2)}) collective-permute-start(bf16[192,2048]{1,0:T(8,128)(2,1)S(1)} %collective-permute-done.16.refs_4_.refs_1_), channel_id=1, source_target_pairs={{4,0},{8,12},{5,1},{9,13},{6,2},{10,14},{7,3},{11,15},{20,16},{24,... | collective-permute-start | bytes 2359304 | tf_op jit(solution)/shard_map/ppermute | solution.py:71
  212.3 35.1 %collective-permute-start.22 = (bf16[192,2048]{1,0:T(8,128)(2,1)}, bf16[192,2048]{1,0:T(8,128)(2,1)}, u32[]{:S(2)}, u32[]{:S(2)}) collective-permute-start(bf16[192,2048]{1,0:T(8,128)(2,1)} %collective-permute-done.19.refs_8_.refs_3_), channel_id=1, source_target_pairs={{4,0},{8,12},{5,1},{9,13},{6,2},{10,14},{7,3},{11,15},{20,16},{24,... | collective-permute-start | bytes 2359304 | tf_op jit(solution)/shard_map/ppermute | solution.py:75
  232.0 58.1 %collective-permute-start.20 = (bf16[256,2048]{1,0:T(8,128)(2,1)}, bf16[256,2048]{1,0:T(8,128)(2,1)}, u32[]{:S(2)}, u32[]{:S(2)}) collective-permute-start(bf16[256,2048]{1,0:T(8,128)(2,1)} %get-tuple-element.93), channel_id=1, source_target_pairs={{0,4},{12,8},{1,5},{13,9},{2,6},{14,10},{3,7},{15,11},{16,20},{28,... | collective-permute-start | bytes 3145736 | tf_op jit(solution)/shard_map/ppermute | solution.py:100
  233.7 74.0 %collective-permute-start.21 = (bf16[256,2048]{1,0:T(8,128)(2,1)S(1)}, bf16[256,2048]{1,0:T(8,128)(2,1)}, u32[]{:S(2)}, u32[]{:S(2)}) collective-permute-start(bf16[256,2048]{1,0:T(8,128)(2,1)S(1)} %add_convert_fusion.3.refs_13_), channel_id=1, source_target_pairs={{4,8},{8,4},{5,9},{9,5},{6,10},{10,6},{7,11},{11,7},{20,24},{24,20... | collective-permute-start | bytes 3145736 | tf_op jit(solution)/shard_map/ppermute | solution.py:101
  283.5 22.7 %all-to-all-start = ((bf16[4,2,128,512]{3,2,1,0:T(8,128)(2,1)}), bf16[4,2,128,512]{3,2,1,0:T(8,128)(2,1)}, u32[]{:S(2)}, u32[]{:S(2)}) async-start(bf16[4,2,128,512]{3,2,1,0:T(8,128)(2,1)} %copy.35), calls=%async_computation | async-start | bytes 2097152 | tf_op jit(solution)/shard_map/all_to_all | solution.py:716
  306.1 21.7 %collective-permute-start.26 = (bf16[128,2048]{1,0:T(8,128)(2,1)}, bf16[128,2048]{1,0:T(8,128)(2,1)}, u32[]{:S(2)}, u32[]{:S(2)}) collective-permute-start(bf16[128,2048]{1,0:T(8,128)(2,1)} %copy-done.34), channel_id=1, source_target_pairs={{0,4},{12,8},{1,5},{13,9},{2,6},{14,10},{3,7},{15,11},{16,20},{28,... | collective-permute-start | bytes 1572872 | tf_op jit(solution)/shard_map/ppermute | solution.py:100
  309.6 55.8 %collective-permute-start.23 = (bf16[256,2048]{1,0:T(8,128)(2,1)S(1)}, bf16[256,2048]{1,0:T(8,128)(2,1)}, u32[]{:S(2)}, u32[]{:S(2)}) collective-permute-start(bf16[256,2048]{1,0:T(8,128)(2,1)S(1)} %add_convert_fusion.2.refs_7_), channel_id=1, source_target_pairs={{4,8},{8,4},{5,9},{9,5},{6,10},{10,6},{7,11},{11,7},{20,24},{24,20... | collective-permute-start | bytes 3145736 | tf_op jit(solution)/shard_map/ppermute | solution.py:108
  312.3 56.5 %collective-permute-start.24 = (bf16[256,2048]{1,0:T(8,128)(2,1)S(1)}, bf16[256,2048]{1,0:T(8,128)(2,1)}, u32[]{:S(2)}, u32[]{:S(2)}) collective-permute-start(bf16[256,2048]{1,0:T(8,128)(2,1)S(1)} %add_convert_fusion.1.refs_8_), channel_id=1, source_target_pairs={{0,4},{4,0},{8,12},{12,8},{1,5},{5,1},{9,13},{13,9},{2,6},{6,2},{1... | collective-permute-start | bytes 3145736 | tf_op jit(solution)/shard_map/ppermute | solution.py:109
  314.7 32.9 %collective-permute-start.27 = (bf16[128,2048]{1,0:T(8,128)(2,1)}, bf16[128,2048]{1,0:T(8,128)(2,1)}, u32[]{:S(2)}, u32[]{:S(2)}) collective-permute-start(bf16[128,2048]{1,0:T(8,128)(2,1)} %add_convert_fusion.7.refs_6_), channel_id=1, source_target_pairs={{4,8},{8,4},{5,9},{9,5},{6,10},{10,6},{7,11},{11,7},{20,24},{24,20... | collective-permute-start | bytes 1572872 | tf_op jit(solution)/shard_map/ppermute | solution.py:101
  349.0 41.5 %collective-permute-start.28 = (bf16[128,2048]{1,0:T(8,128)(2,1)S(1)}, bf16[128,2048]{1,0:T(8,128)(2,1)S(1)}, u32[]{:S(2)}, u32[]{:S(2)}) collective-permute-start(bf16[128,2048]{1,0:T(8,128)(2,1)S(1)} %add_convert_fusion.6.refs_3_), channel_id=1, source_target_pairs={{4,8},{8,4},{5,9},{9,5},{6,10},{10,6},{7,11},{11,7},{20,24},{24,20... | collective-permute-start | bytes 1572872 | tf_op jit(solution)/shard_map/ppermute | solution.py:108
  352.0 38.4 %collective-permute-start.29 = (bf16[128,2048]{1,0:T(8,128)(2,1)S(1)}, bf16[128,2048]{1,0:T(8,128)(2,1)S(1)}, u32[]{:S(2)}, u32[]{:S(2)}) collective-permute-start(bf16[128,2048]{1,0:T(8,128)(2,1)S(1)} %add_convert_fusion.5.refs_4_), channel_id=1, source_target_pairs={{0,4},{4,0},{8,12},{12,8},{1,5},{5,1},{9,13},{13,9},{2,6},{6,2},{1... | collective-permute-start | bytes 1572872 | tf_op jit(solution)/shard_map/ppermute | solution.py:109
  365.5 21.1 %collective-permute-start.31 = (bf16[64,2048]{1,0:T(8,128)(2,1)S(1)}, bf16[64,2048]{1,0:T(8,128)(2,1)S(1)}, u32[]{:S(2)}, u32[]{:S(2)}) collective-permute-start(bf16[64,2048]{1,0:T(8,128)(2,1)S(1)} %get-tuple-element.114), channel_id=1, source_target_pairs={{0,8},{4,12},{8,0},{12,4},{1,9},{5,13},{9,1},{13,5},{2,10},{6,14},... | collective-permute-start | bytes 786440 | tf_op jit(solution)/shard_map/ppermute | solution.py:753
  368.8 20.7 %collective-permute-start.32 = (bf16[64,2048]{1,0:T(8,128)(2,1)S(1)}, bf16[64,2048]{1,0:T(8,128)(2,1)S(1)}, u32[]{:S(2)}, u32[]{:S(2)}) collective-permute-start(bf16[64,2048]{1,0:T(8,128)(2,1)S(1)} %get-tuple-element.115), channel_id=1, source_target_pairs={{0,12},{4,0},{8,4},{12,8},{1,13},{5,1},{9,5},{13,9},{2,14},{6,2},{... | collective-permute-start | bytes 786440 | tf_op jit(solution)/shard_map/ppermute | solution.py:753
  (62 other events, 673.6 us)
